TPU v7x, 256 devices: a whole 4x4x8 slice. The times are simulated.
256 devices in a mesh: patch: 8 (over z), expert: 16 (over y, x), hidden: 2 (over core).
Axes of the slice: x: 4, y: 4, z: 8, core: 2. Of those that a mesh axis runs over, the one named last changes fastest.
Arguments:
- tokens: bfloat16 [16384, 4096], P(('patch', 'expert')), may hold values from -6 to 6
- cotangent: bfloat16 [16384, 4096], P(('patch', 'expert')), may hold values from -1.5 to 1.5
- w_in: bfloat16 [16, 4096, 4096], P('expert', None, ('patch', 'hidden')), may hold values from -0.09375 to 0.09375
- w_out: bfloat16 [16, 4096, 4096], P('expert', ('patch', 'hidden')), may hold values from -0.09375 to 0.09375
- gates: float32 [16, 1024], P('expert'), may hold values from 0.1 to 1
- picks: int32 [16, 1024], replicated, may hold values from 0 to 16383, as said below
- counts: int32 [16], replicated, may hold values from 512 to 1024, as said below
Outputs:
- d_tokens: bfloat16 [16384, 4096], P(('patch', 'expert'), 'hidden')
- d_w_in: bfloat16 [16, 4096, 4096], P('expert', None, ('patch', 'hidden'))
- d_w_out: bfloat16 [16, 4096, 4096], P('expert', ('patch', 'hidden'))
- d_gates: float32 [16, 1024], P('expert', ('patch', 'hidden'))
Inputs may be any that keep to these rules, and one draw needn't show every extreme that they name: `picks`: each expert's list names distinct rows. Slots from counts[e] on are padding and name rows that are ignored. Within one expert's aligned block of 128 slots, at most 2 slots name rows of one aligned block of 128 rows, and this bound is reached in every draw. `counts`: some expert has all 1024 slots live.
All inputs are finite; a program needn't handle non-finite values.
Results may differ from a plain program's by a relative error of at most 0.023.
Values may be sent and summed in bfloat16 or wider, within the bound.
A program may use at most 128 MiB of HBM per device.

v0:
```python
import jax
import jax.numpy as jnp
from jax import lax
from jax.sharding import PartitionSpec as P

inv_root_two = 0.7071067811865476
inv_root_two_pi = 0.3989422804014327


def gelu_parts(pre):
    normal_cdf = 0.5 * (1.0 + lax.erf(pre * inv_root_two))
    density = jnp.exp(-0.5 * pre * pre) * inv_root_two_pi
    return (pre * normal_cdf, normal_cdf + pre * density)


def local(tokens, cotangent, w_in, w_out, gates, picks, counts):
    tok_dev, width = tokens.shape
    patch_count = lax.axis_size("patch")
    expert_count = lax.axis_size("expert")
    hidden_parts = lax.axis_size("hidden")
    capacity = picks.shape[1]
    slots = capacity // patch_count
    sources = patch_count * expert_count
    bound = 2 * max(1, slots // sources)
    limit = sources * bound
    patch_here = lax.axis_index("patch")
    expert_here = lax.axis_index("expert")
    source_here = patch_here * expert_count + expert_here
    slot_ids = jnp.arange(capacity, dtype=jnp.int32)
    live = slot_ids[None, :] < counts[:, None]
    holder = picks // tok_dev
    local_row = picks % tok_dev
    mine = (
        ((holder == source_here) & live).reshape(expert_count, patch_count, slots).astype(jnp.int32)
    )
    order_mine = jnp.cumsum(mine, axis=2) - 1
    expert_ids = jnp.arange(expert_count, dtype=jnp.int32)[:, None, None]
    patch_ids = jnp.arange(patch_count, dtype=jnp.int32)[None, :, None]
    position = (patch_ids * expert_count + expert_ids) * bound + order_mine
    position = jnp.where(mine == 1, position, limit)
    send_table = (
        jnp.full((limit,), tok_dev, jnp.int32)
        .at[position.reshape(-1)]
        .set(local_row.reshape(-1), mode="drop")
    )
    send_rows = jnp.take(tokens, send_table, axis=0, mode="fill", fill_value=0).reshape(
        sources, bound, width
    )
    send_grads = jnp.take(cotangent, send_table, axis=0, mode="fill", fill_value=0).reshape(
        sources, bound, width
    )
    came_rows, came_grads = (
        lax.all_to_all(send_rows, ("patch", "expert"), split_axis=0, concat_axis=0, tiled=True),
        lax.all_to_all(send_grads, ("patch", "expert"), split_axis=0, concat_axis=0, tiled=True),
    )
    my_picks = lax.dynamic_slice_in_dim(picks, expert_here, 1, 0)[0]
    block_picks = lax.dynamic_slice_in_dim(my_picks, patch_here * slots, slots, 0)
    count_here = lax.dynamic_slice_in_dim(counts, expert_here, 1, 0)[0]
    within = jnp.arange(slots, dtype=jnp.int32)
    block_live = patch_here * slots + within < count_here
    block_holder = block_picks // tok_dev
    earlier_same = (
        (block_holder[:, None] == block_holder[None, :])
        & block_live[None, :]
        & (within[None, :] < within[:, None])
    )
    block_order = jnp.sum(earlier_same.astype(jnp.int32), axis=1)
    came_index = jnp.where(block_live, block_holder * bound + block_order, limit)
    block_rows = jnp.take(
        came_rows.reshape(limit, width), came_index, axis=0, mode="fill", fill_value=0
    )
    block_grads = jnp.take(
        came_grads.reshape(limit, width), came_index, axis=0, mode="fill", fill_value=0
    )
    slot_rows, grad_rows = (
        lax.all_gather(block_rows, "patch", axis=0, tiled=True),
        lax.all_gather(block_grads, "patch", axis=0, tiled=True),
    )
    gate_col = gates[0][:, None]
    weight_in = w_in[0]
    weight_out = w_out[0]
    unit_count = weight_in.shape[1]
    pre = jnp.dot(slot_rows, weight_in, preferred_element_type=jnp.float32)
    act, slope = gelu_parts(pre)
    act_b = act.astype(jnp.bfloat16)
    back_act = lax.dot_general(
        grad_rows, weight_out, (((1,), (1,)), ((), ())), preferred_element_type=jnp.float32
    )
    gate_grad = jnp.sum(act * back_act, axis=1)
    back_pre = (gate_col * back_act * slope).astype(jnp.bfloat16)
    gated_rows = (gate_col * grad_rows.astype(jnp.float32)).astype(jnp.bfloat16)
    grad_in = lax.dot_general(
        slot_rows, back_pre, (((0,), (0,)), ((), ())), preferred_element_type=jnp.float32
    )
    grad_out = lax.dot_general(
        act_b, gated_rows, (((0,), (0,)), ((), ())), preferred_element_type=jnp.float32
    )
    gate_terms = gate_grad.reshape(patch_count * hidden_parts, slots // hidden_parts)
    d_gates = lax.psum_scatter(gate_terms, ("patch", "hidden"), scatter_dimension=0, tiled=True)
    selector = (jnp.arange(tok_dev, dtype=jnp.int32)[:, None] == send_table[None, :]).astype(
        jnp.bfloat16
    )
    back_blocks = back_pre.reshape(patch_count, slots, unit_count)
    weight_halves = weight_in.reshape(hidden_parts, width // hidden_parts, unit_count)
    slot_terms = jnp.einsum(
        "psf,hdf->phsd", back_blocks, weight_halves, preferred_element_type=jnp.float32
    ).astype(jnp.bfloat16)
    slot_terms = slot_terms.reshape(patch_count * hidden_parts, slots, width // hidden_parts)
    slot_sum = lax.psum_scatter(
        slot_terms, ("patch", "hidden"), scatter_dimension=0, tiled=True
    ).astype(jnp.float32)[0]
    slot_grad = slot_sum.astype(jnp.bfloat16)
    going_back = (
        jnp.zeros((limit, width // hidden_parts), jnp.bfloat16)
        .at[came_index]
        .set(slot_grad, mode="drop")
    )
    send_width = width // hidden_parts
    returned = lax.all_to_all(
        going_back.reshape(sources, bound, send_width),
        ("patch", "expert"),
        split_axis=0,
        concat_axis=0,
        tiled=True,
    )
    returned = returned.reshape(limit, send_width)
    token_grad = jnp.dot(selector, returned, preferred_element_type=jnp.float32)
    d_tokens = token_grad.astype(jnp.bfloat16)
    return (
        d_tokens,
        grad_in.astype(jnp.bfloat16)[None],
        grad_out.astype(jnp.bfloat16)[None],
        d_gates,
    )


def solution(mesh):
    in_specs = (
        P(("patch", "expert"), None),
        P(("patch", "expert"), None),
        P("expert", None, ("patch", "hidden")),
        P("expert", ("patch", "hidden"), None),
        P("expert", None),
        P(),
        P(),
    )
    out_specs = (
        P(("patch", "expert"), "hidden"),
        P("expert", None, ("patch", "hidden")),
        P("expert", ("patch", "hidden"), None),
        P("expert", ("patch", "hidden")),
    )
    return jax.shard_map(local, mesh=mesh, in_specs=in_specs, out_specs=out_specs, check_vma=False)
```

profile of v0, /device:TPU:4, one launch (start us, length us, event | category | flops | bytes accessed | tf_op | source)
XLA Modules:
  0.0 582.4 jit_solution(9173325607399050647)
XLA Ops:
  7.2 1.0 fusion.21
  8.3 0.9 convert_bitcast_fusion
  9.3 0.1 copy.12
  9.4 4.5 reduce_window_sum.11
  13.9 0.1 add_add_fusion
  14.0 0.1 compare_select_fusion
  14.1 60.3 %scatter_custom_fusion = s32[256]{0:T(256)S(1)} fusion(s32[16384]{0:T(1024)S(1)} %bitcast.87, s32[16384]{0:T(1024)S(1)} %bitcast.88, s32[]{:T(128)} %constant.94.clone.1), kind=kCustom, calls=%fused_computation.87 | custom fusion | bytes 1028 | tf_op jit(solution)/shard_map/scatter | solution.py:44
  74.5 3.2 gather_fusion.2
  77.6 6.6 %gather_fusion = bf16[256,4096]{1,0:T(8,128)(2,1)} fusion(bf16[128,4096]{1,0:T(8,128)(2,1)} %param.12, s32[1024]{0:T(1024)S(1)} %pad_clamp_fusion.1), kind=kCustom, calls=%fused_computation.clone | custom fusion | bytes 4195328 | tf_op jit(solution)/shard_map/jit(_take)/gather | solution.py:49
  84.2 4.6 broadcast_select_fusion.1
  88.8 4.4 reshape.258
  93.2 15.9 %all-to-all-start = ((bf16[128,2,4096]{2,1,0:T(2,128)(2,1)}), bf16[128,2,4096]{2,1,0:T(2,128)(2,1)}, u32[]{:S(2)}, u32[]{:S(2)}) async-start(bf16[128,2,4096]{2,1,0:T(2,128)(2,1)} %reshape.258), calls=%async_computation | async-start | bytes 4194304 | tf_op jit(solution)/shard_map/all_to_all | solution.py:54
  109.0 4.4 reshape.260
  113.4 46.1 %all-to-all-done = bf16[128,2,4096]{2,1,0:T(2,128)(2,1)} async-done(((bf16[128,2,4096]{2,1,0:T(2,128)(2,1)}), bf16[128,2,4096]{2,1,0:T(2,128)(2,1)}, u32[]{:S(2)}, u32[]{:S(2)}) %all-to-all-start) | async-done | bytes 2097184 | tf_op jit(solution)/shard_map/all_to_all | solution.py:54
  159.5 9.5 %all-to-all-start.1 = ((bf16[128,2,4096]{2,1,0:T(2,128)(2,1)}), bf16[128,2,4096]{2,1,0:T(2,128)(2,1)}, u32[]{:S(2)}, u32[]{:S(2)}) async-start(bf16[128,2,4096]{2,1,0:T(2,128)(2,1)} %reshape.260), calls=%async_computation.1 | async-start | bytes 4194304 | tf_op jit(solution)/shard_map/all_to_all | solution.py:53
  169.0 0.2 all-gather.5.cloned.1.call-start
  169.2 0.6 dynamic_slice.11
  169.8 0.7 add_compare_fusion
  170.5 0.8 and_select_fusion.1
  171.3 0.2 convert_reduce_fusion
  171.5 0.7 compare_and_fusion
  172.1 4.1 reshape.259
  176.2 4.1 gather_fusion.1
  180.3 38.4 %all-to-all-done.1 = bf16[128,2,4096]{2,1,0:T(2,128)(2,1)} async-done(((bf16[128,2,4096]{2,1,0:T(2,128)(2,1)}), bf16[128,2,4096]{2,1,0:T(2,128)(2,1)}, u32[]{:S(2)}, u32[]{:S(2)}) %all-to-all-start.1) | async-done | bytes 2097184 | tf_op jit(solution)/shard_map/all_to_all | solution.py:53
  218.7 4.1 reshape.261
  222.8 5.0 gather_fusion.3
  227.8 2.7 broadcast_select_fusion.3
  230.6 0.0 all-gather.3.cloned.1.call-start
  230.6 0.7 all-gather.3.cloned.1.call-update
  231.3 0.0 reduce-scatter.2.cloned.1.call-start
  231.4 90.0 %all-gather.5.cloned.1.call-done = bf16[1024,4096]{1,0:T(8,128)(2,1)} async-done(((bf16[128,4096]{1,0:T(8,128)(2,1)}), bf16[1024,4096]{1,0:T(8,128)(2,1)}) %all-gather.5.cloned.1.call-update) | async-done | bytes 8388624 | tf_op jit(solution)/shard_map/all_gather | solution.py:76
  321.4 5.7 fusion.5
  327.1 89.4 %all-gather.3.cloned.1.call-done = bf16[1024,4096]{1,0:T(8,128)(2,1)} async-done(((bf16[128,4096]{1,0:T(8,128)(2,1)}), bf16[1024,4096]{1,0:T(8,128)(2,1)}) %all-gather.3.cloned.1.call-update) | async-done | bytes 8388624 | tf_op jit(solution)/shard_map/all_gather | solution.py:77
  416.5 6.7 %multiply_reduce_fusion = (f32[1024]{0:T(1024)S(1)}, bf16[1024,256]{1,0:T(8,128)(2,1)S(1)}) fusion(f32[1024,256]{1,0:T(8,128)S(1)} %fusion.5, f32[1024]{0:T(1024)S(1)} %bitcast.89, bf16[1024,4096]{1,0:T(8,128)(2,1)} %all-gather.3.cloned.1.call-done, bf16[1,256,4096]{2,1,0:T(8,128)(2,1)} %param.14), kind=kOutput, calls=%fused_computation.28 | convolution fusion | flops 2151152640 | bytes 12066816 | tf_op jit(solution)/shard_map/dot_general | solution.py:86
  423.2 5.6 convolution_convert_fusion
  428.9 0.7 fusion.31
  429.5 68.7 %reduce-scatter.2.cloned.1.call-done = bf16[1,128,2048]{2,1,0:T(8,128)(2,1)} async-done(((bf16[16,128,2048]{2,1,0:T(8,128)(2,1)}), bf16[1,128,2048]{2,1,0:T(8,128)(2,1)}) %reduce-scatter.2.cloned.1.call-update) | async-done | bytes 524304 | tf_op jit(solution)/shard_map/reduce_scatter | solution.py:109
  498.3 2.2 scatter_custom_fusion.1
  500.5 1.5 reshape.264
  502.0 11.3 %all-to-all-start.2 = ((bf16[128,2,2048]{2,1,0:T(2,128)(2,1)}), bf16[128,2,2048]{2,1,0:T(2,128)(2,1)S(1)}, u32[]{:S(2)}, u32[]{:S(2)}) async-start(bf16[128,2,2048]{2,1,0:T(2,128)(2,1)} %reshape.264), calls=%async_computation.3 | async-start | bytes 2097152 | tf_op jit(solution)/shard_map/all_to_all | solution.py:119
  513.3 0.6 dynamic-slice.1
  513.9 0.1 reshape.266
  514.0 42.0 %all-reduce = f32[16,64]{1,0:T(8,128)S(1)} all-reduce(f32[16,64]{1,0:T(8,128)S(1)} %reshape.266), channel_id=3, replica_groups=mesh['patch'=8,'expert'=16,'hidden'=2] {'patch','hidden'}, use_global_device_ids=true, to_apply=%region_6.9.clone | all-reduce | flops 1024 | bytes 8192
  556.0 1.2 constant_dynamic-slice_fusion
  557.2 7.9 %fusion.3 = bf16[1,256,4096]{2,1,0:T(8,128)(2,1)} fusion(bf16[1024,4096]{1,0:T(8,128)(2,1)} %all-gather.3.cloned.1.call-done, f32[1024]{0:T(1024)S(1)} %bitcast.90, f32[1024,256]{1,0:T(8,128)} %copy-done.7), kind=kOutput, calls=%fused_computation.12 | convolution fusion | flops 2162425856 | bytes 11538432 | tf_op jit(solution)/shard_map/dot_general | solution.py:95
  565.1 7.2 %fusion.4 = bf16[1,4096,256]{2,1,0:T(8,128)(2,1)} fusion(bf16[1024,4096]{1,0:T(8,128)(2,1)} %all-gather.5.cloned.1.call-done, bf16[1024,256]{1,0:T(8,128)(2,1)S(1)} %copy-done.3), kind=kOutput, calls=%fused_computation.13 | convolution fusion | flops 2148532224 | bytes 11010048 | tf_op jit(solution)/shard_map/dot_general | solution.py:92
  572.3 1.2 reshape.265
  573.5 2.3 convolution_convert_fusion.2
  (29 shorter events, 0.2 us)
Async XLA Ops:
  7.2 314.2 %copy-start = (bf16[1,4096,256]{2,1,0:T(8,128)(2,1)S(1)}, bf16[1,4096,256]{2,1,0:T(8,128)(2,1)}, u32[]{:S(2)}) copy-start(bf16[1,4096,256]{2,1,0:T(8,128)(2,1)} %param.13) | copy-start | bytes 6291460
  7.2 67.3 %copy-start.1 = (bf16[128,4096]{1,0:T(8,128)(2,1)S(1)}, bf16[128,4096]{1,0:T(8,128)(2,1)}, u32[]{:S(2)}) copy-start(bf16[128,4096]{1,0:T(8,128)(2,1)} %param.11) | copy-start | bytes 3145732
  93.2 66.3 %all-to-all-start = ((bf16[128,2,4096]{2,1,0:T(2,128)(2,1)}), bf16[128,2,4096]{2,1,0:T(2,128)(2,1)}, u32[]{:S(2)}, u32[]{:S(2)}) async-start(bf16[128,2,4096]{2,1,0:T(2,128)(2,1)} %reshape.258), calls=%async_computation | async-start | bytes 4194304 | tf_op jit(solution)/shard_map/all_to_all | solution.py:54
  113.4 55.8 %copy-start.4 = (s32[16]{0:T(128)S(1)}, s32[16]{0:T(128)}, u32[]{:S(2)}) copy-start(s32[16]{0:T(128)} %param.17) | copy-start | bytes 196
  159.5 59.2 %all-to-all-start.1 = ((bf16[128,2,4096]{2,1,0:T(2,128)(2,1)}), bf16[128,2,4096]{2,1,0:T(2,128)(2,1)}, u32[]{:S(2)}, u32[]{:S(2)}) async-start(bf16[128,2,4096]{2,1,0:T(2,128)(2,1)} %reshape.260), calls=%async_computation.1 | async-start | bytes 4194304 | tf_op jit(solution)/shard_map/all_to_all | solution.py:53
  169.0 152.4 %all-gather.5.cloned.1.call-start = ((), (), s32[]{:S(2)}) async-start(), calls=%async_computation.5 | async-start | bytes 9437184 | tf_op jit(solution)/shard_map/all_gather | solution.py:76
  230.6 185.9 %all-gather.3.cloned.1.call-start = ((), (), s32[]{:S(2)}) async-start(), calls=%async_computation.4 | async-start | bytes 9437184 | tf_op jit(solution)/shard_map/all_gather | solution.py:77
  231.3 185.2 %copy-start.5 = (f32[1,1024]{1,0:T(1,128)S(1)}, f32[1,1024]{1,0:T(1,128)}, u32[]{:S(2)}) copy-start(f32[1,1024]{1,0:T(1,128)} %param.15) | copy-start | bytes 12292
  231.3 266.9 %reduce-scatter.2.cloned.1.call-start = ((), (), s32[]{:S(2)}) async-start(), calls=%async_computation.6 | async-start | bytes 8912896 | tf_op jit(solution)/shard_map/reduce_scatter | solution.py:109
  327.1 96.1 %copy-start.7 = (f32[1024,256]{1,0:T(8,128)}, f32[1024,256]{1,0:T(8,128)S(1)}, u32[]{:S(2)}) copy-start(f32[1024,256]{1,0:T(8,128)S(1)} %fusion.5) | copy-start | bytes 3145732
  423.2 5.6 copy-start.2
  500.5 12.8 %copy-start.6 = (u32[256]{0:T(256)S(1)}, u32[256]{0:T(256)}, u32[]{:S(2)}) copy-start(u32[256]{0:T(256)} %constant.122) | copy-start | bytes 3076
  502.0 70.4 %all-to-all-start.2 = ((bf16[128,2,2048]{2,1,0:T(2,128)(2,1)}), bf16[128,2,2048]{2,1,0:T(2,128)(2,1)S(1)}, u32[]{:S(2)}, u32[]{:S(2)}) async-start(bf16[128,2,2048]{2,1,0:T(2,128)(2,1)} %reshape.264), calls=%async_computation.3 | async-start | bytes 2097152 | tf_op jit(solution)/shard_map/all_to_all | solution.py:119
  557.2 7.9 %copy-start.3 = (bf16[1024,256]{1,0:T(8,128)(2,1)S(1)}, bf16[1024,256]{1,0:T(8,128)(2,1)}, u32[]{:S(2)}) copy-start(bf16[1024,256]{1,0:T(8,128)(2,1)} %copy-done.2) | copy-start | bytes 1572868
Sparse Core Ops, SparseCore 0:
  230.7 90.6 all-gather.4
  323.7 92.7 all-gather.2
  429.0 69.2 reduce-scatter.1
where the time goes:
time: 584 us; the launch traced here: 582 us
  waiting for transfers between devices  333 us (57%)
  local copies, waits for them, and re-layouts  104 us (18%)
  blocking collectives  42 us (7%)
  starting transfers between devices  37 us (6%)
  matrix products  35.5 us (6%)
  other arithmetic  17 us (3%)
  between operations  14 us (2%)
    all_gather x1, waiting for transfers between devices, local(): lax.all_gather(block_rows, 'patch', axis=0, tiled=True)  90 us
    all_gather x1, waiting for transfers between devices, local(): lax.all_gather(block_grads, 'patch', axis=0, tiled=True)  89.4 us
    reduce_scatter x1, waiting for transfers between devices, local(): lax.psum_scatter(slot_terms, ('patch', 'hidden'), scatter_dimension=0, ti...  68.7 us
    scatter x1, local copies, waits for them, and re-layouts, local(): send_table = jnp.full((limit,), tok_dev, jnp.int32).at[position.reshape(-...  60.3 us
    all_to_all x1, waiting for transfers between devices, local(): lax.all_to_all(send_grads, ('patch', 'expert'), split_axis=0, concat_axis...  46.1 us
    unnamed x1, blocking collectives  42 us
    all_to_all x1, waiting for transfers between devices, local(): lax.all_to_all(send_rows, ('patch', 'expert'), split_axis=0, concat_axis=...  38.4 us
    all_to_all x1, starting transfers between devices, local(): lax.all_to_all(send_grads, ('patch', 'expert'), split_axis=0, concat_axis...  15.9 us
  transfers between devices with their start and end apart: 6, of which 5 were waited for; matrix products, arithmetic and copies ran while one was open for 7% of the time, Pallas kernels for 0%

commit v1 on v0

--- a/solution.py
+++ b/solution.py
@@ -1,6 +1,10 @@
+import functools
+
 import jax
 import jax.numpy as jnp
 from jax import lax
+from jax.experimental import pallas as pl
+from jax.experimental.pallas import tpu as pltpu
 from jax.sharding import PartitionSpec as P
 
 inv_root_two = 0.7071067811865476
@@ -13,7 +17,7 @@
     return (pre * normal_cdf, normal_cdf + pre * density)
 
 
-def local(tokens, cotangent, w_in, w_out, gates, picks, counts):
+def general(tokens, cotangent, w_in, w_out, gates, picks, counts):
     tok_dev, width = tokens.shape
     patch_count = lax.axis_size("patch")
     expert_count = lax.axis_size("expert")
@@ -134,6 +138,525 @@
     )
 
 
+MESH = pl.DeviceIdType.MESH
+f32 = jnp.float32
+bf16 = jnp.bfloat16
+ROWS_PER_PAIR = 16
+PIECES = 4
+
+
+def contract(a, b, dim_a, dim_b):
+    return lax.dot_general(a, b, (((dim_a,), (dim_b,)), ((), ())), preferred_element_type=f32)
+
+
+def row_sums(x):
+    ones = jnp.ones((8, x.shape[1]), bf16)
+    high = x.astype(bf16)
+    low = (x - high.astype(f32)).astype(bf16)
+    return (contract(ones, high, 1, 1) + contract(ones, low, 1, 1))[0:1]
+
+
+def kernel(
+    planes,
+    experts,
+    cap,
+    tokens,
+    cotangent,
+    w_in_hbm,
+    w_out_hbm,
+    pick_sel,
+    pack_sel,
+    gate_ref,
+    d_tok_hbm,
+    d_in_hbm,
+    d_out_hbm,
+    gate_total,
+    held,
+    going,
+    came,
+    allrows,
+    win,
+    wout,
+    act_s,
+    back_s,
+    home,
+    part_out,
+    part_in,
+    sum_out,
+    sum_in,
+    grad_go,
+    grad_came,
+    d_tok,
+    d_in,
+    d_out,
+    gate_lo,
+    gate_hi,
+    gate_all,
+    load_sem,
+    go_send,
+    go_recv,
+    ring_send,
+    ring_recv,
+    twin_send,
+    twin_recv,
+    part_send,
+    part_recv,
+    sum_send,
+    sum_recv,
+    grad_send,
+    grad_recv,
+    gate_send,
+    gate_recv,
+    store_sem,
+):
+    z = lax.axis_index("patch")
+    e = lax.axis_index("expert")
+    c = lax.axis_index("hidden")
+    other = 1 - c
+    up = (lax.rem(z + 1, planes), e, c)
+    down = (lax.rem(z + planes - 1, planes), e, c)
+    twin = (z, e, other)
+    width = PIECES * held.shape[3]
+    piece = held.shape[3]
+    half = cap // 2
+    plane_peers = [(z, lax.rem(e + k, experts), c) for k in range(1, experts)]
+    me = z * 2 + c
+    column_ids = [lax.rem(me + k, 2 * planes) for k in range(1, 2 * planes)]
+    column_peers = [(i // 2, e, lax.rem(i, 2)) for i in column_ids]
+
+    barrier = pltpu.get_barrier_semaphore()
+    for peer in plane_peers + column_peers:
+        pl.semaphore_signal(barrier, inc=1, device_id=peer, device_id_type=MESH)
+
+    loads = []
+    for a, ref in enumerate((tokens, cotangent)):
+        for j in range(2):
+            col = pl.multiple_of((2 * c + j) * piece, piece)
+            cp = pltpu.make_async_copy(
+                ref.at[:, pl.ds(col, piece)], held.at[a, j], load_sem.at[2 * a + j]
+            )
+            cp.start()
+            loads.append(cp)
+    load_in = pltpu.make_async_copy(w_in_hbm, win, load_sem.at[4])
+    load_out = pltpu.make_async_copy(w_out_hbm, wout, load_sem.at[5])
+    load_in.start()
+    load_out.start()
+
+    pl.semaphore_wait(barrier, len(plane_peers) + len(column_peers))
+
+    def remote(src, dst, s, r, dev):
+        return pltpu.make_async_remote_copy(
+            src_ref=src, dst_ref=dst, send_sem=s, recv_sem=r, device_id=dev, device_id_type=MESH
+        )
+
+    def plane_copy(src, dst, ssem, rsem, k):
+        to = pl.multiple_of(lax.rem(e + k, experts) * ROWS_PER_PAIR, ROWS_PER_PAIR)
+        at = pl.multiple_of(e * ROWS_PER_PAIR, ROWS_PER_PAIR)
+        return remote(
+            src.at[pl.ds(to, ROWS_PER_PAIR)],
+            dst.at[pl.ds(at, ROWS_PER_PAIR)],
+            ssem.at[k],
+            rsem.at[k],
+            plane_peers[k - 1],
+        )
+
+    own_rows = pl.ds(pl.multiple_of(e * ROWS_PER_PAIR, ROWS_PER_PAIR), ROWS_PER_PAIR)
+
+    for a in range(2):
+        for j in range(2):
+            loads[2 * a + j].wait()
+            going[a, j] = contract(pick_sel[...], held[a, j], 1, 0).astype(bf16)
+            came[a, j, own_rows, :] = going[a, j, own_rows, :]
+            for k in range(1, experts):
+                plane_copy(
+                    going.at[a, j], came.at[a, j], go_send.at[a, j], go_recv.at[a, j], k
+                ).start()
+
+    def ring_up(a, j, t):
+        q = 2 * c + j
+        return remote(
+            allrows.at[a, q, t, pl.ds(0, half)],
+            allrows.at[a, q, t + 1, pl.ds(0, half)],
+            ring_send.at[0, a, j, t],
+            ring_recv.at[0, a, j, t + 1],
+            up,
+        )
+
+    def ring_down(a, j, t):
+        q = 2 * c + j
+        return remote(
+            allrows.at[a, q, t, pl.ds(half, half)],
+            allrows.at[a, q, t + 1, pl.ds(half, half)],
+            ring_send.at[1, a, j, t],
+            ring_recv.at[1, a, j, t + 1],
+            down,
+        )
+
+    def twin_copy(a, j, t):
+        q = 2 * c + j
+        return remote(
+            allrows.at[a, q, t],
+            allrows.at[a, q, t],
+            twin_send.at[a, j, t],
+            twin_recv.at[a, j, t],
+            twin,
+        )
+
+    def part_copy(j, t):
+        slot = lax.rem(t, 2)
+        return remote(
+            part_out.at[slot, j], part_in.at[t, j], part_send.at[t, j], part_recv.at[t, j], twin
+        )
+
+    def sum_up(j, t):
+        return remote(
+            sum_out.at[lax.rem(t, 2), j, pl.ds(0, half)],
+            sum_in.at[t, j, pl.ds(0, half)],
+            sum_send.at[0, j, t],
+            sum_recv.at[0, j, t],
+            up,
+        )
+
+    def sum_down(j, t):
+        return remote(
+            sum_out.at[lax.rem(t, 2), j, pl.ds(half, half)],
+            sum_in.at[t, j, pl.ds(half, half)],
+            sum_send.at[1, j, t],
+            sum_recv.at[1, j, t],
+            down,
+        )
+
+    for a in range(2):
+        for j in range(2):
+            for k in range(1, experts):
+                plane_copy(
+                    going.at[a, j], came.at[a, j], go_send.at[a, j], go_recv.at[a, j], k
+                ).wait()
+            allrows[a, 2 * c + j, 0] = contract(pack_sel[...], came[a, j], 1, 0).astype(bf16)
+            ring_up(a, j, 0).start()
+            ring_down(a, j, 0).start()
+            twin_copy(a, j, 0).start()
+    load_in.wait()
+    load_out.wait()
+
+    def step(t, carry):
+        for a in range(2):
+            for j in range(2):
+
+                @pl.when(t > 0)
+                def _():
+                    ring_up(a, j, t - 1).wait_recv()
+
+                    @pl.when(t < planes - 1)
+                    def _():
+                        ring_up(a, j, t).start()
+
+                    ring_down(a, j, t - 1).wait_recv()
+
+                    @pl.when(t < planes - 1)
+                    def _():
+                        ring_down(a, j, t).start()
+
+                    twin_copy(a, j, t).start()
+
+        for a in range(2):
+            for j in range(2):
+                twin_copy(a, j, t).wait_recv()
+        pre = contract(allrows[0, 0, t], win[0], 1, 0)
+        back = contract(allrows[1, 0, t], wout[:, 0:piece], 1, 1)
+        for q in range(1, PIECES):
+            pre += contract(allrows[0, q, t], win[q], 1, 0)
+            back += contract(allrows[1, q, t], wout[:, q * piece : (q + 1) * piece], 1, 1)
+        act, slope = gelu_parts(pre)
+        gate = gate_ref[t]
+        act_s[t] = (gate * act).astype(bf16)
+        back_pre = (gate * back * slope).astype(bf16)
+        back_s[t] = back_pre
+        gate_row = row_sums(act * back)
+        gate_lo[pl.ds(lax.rem(z + planes - t, planes), 1), 0:cap] = gate_row
+        gate_hi[pl.ds(lax.rem(z + t, planes), 1), 0:cap] = gate_row
+
+        for j in range(2):
+
+            @pl.when(t > 1)
+            def _():
+                part_copy(j, t - 2).wait_send()
+
+            part_out[lax.rem(t, 2), j] = contract(back_pre, win[2 * other + j], 1, 1).astype(bf16)
+            part_copy(j, t).start()
+        for j in range(2):
+            own = contract(back_pre, win[2 * c + j], 1, 1)
+            part_copy(j, t).wait_recv()
+            own += part_in[t, j].astype(f32)
+
+            @pl.when(t == 0)
+            def _():
+                home[j] = own
+
+            @pl.when(t > 2)
+            def _():
+                sum_up(j, t - 2).wait_send()
+                sum_down(j, t - 2).wait_send()
+
+            @pl.when(t > 1)
+            def _():
+                sum_up(j, t - 1).wait_recv()
+                sum_down(j, t - 1).wait_recv()
+                sum_out[lax.rem(t, 2), j] = (own + sum_in[t - 1, j].astype(f32)).astype(bf16)
+
+            @pl.when(t == 1)
+            def _():
+                sum_out[lax.rem(t, 2), j] = own.astype(bf16)
+
+            @pl.when(t > 0)
+            def _():
+                sum_up(j, t).start()
+                sum_down(j, t).start()
+
+        return carry
+
+    lax.fori_loop(0, planes, step, 0)
+
+    lane = lax.broadcasted_iota(jnp.int32, gate_lo.shape, 1)
+    gate_all[me] = jnp.where(
+        lane < half, gate_lo[...], jnp.where(lane < cap, gate_hi[...], 0.0)
+    )
+
+    def gate_copy(k):
+        return remote(
+            gate_all.at[me], gate_all.at[me], gate_send.at[k], gate_recv.at[k], column_peers[k - 1]
+        )
+
+    for k in range(1, 2 * planes):
+        gate_copy(k).start()
+
+    rows = planes * cap
+    act_all = act_s[...].reshape(rows, act_s.shape[2])
+    for q in range(PIECES):
+        d_out[q] = contract(act_all, allrows[1, q].reshape(rows, piece), 0, 0).astype(bf16)
+
+    last = planes - 1
+    for j in range(2):
+        sum_up(j, last).wait_recv()
+        sum_down(j, last).wait_recv()
+        slot_grad = (home[j] + sum_in[last, j].astype(f32)).astype(bf16)
+        grad_go[j] = contract(pack_sel[...], slot_grad, 0, 0).astype(bf16)
+        grad_came[j, own_rows, :] = grad_go[j, own_rows, :]
+        for k in range(1, experts):
+            plane_copy(grad_go.at[j], grad_came.at[j], grad_send.at[j], grad_recv.at[j], k).start()
+
+    stores = []
+    for q in range(PIECES):
+        cp = pltpu.make_async_copy(
+            d_out.at[q], d_out_hbm.at[:, pl.ds(q * piece, piece)], store_sem.at[q]
+        )
+        cp.start()
+        stores.append(cp)
+    back_all = back_s[...].reshape(rows, back_s.shape[2])
+    for q in range(PIECES):
+        turned = contract(back_all, allrows[0, q].reshape(rows, piece), 0, 0)
+        d_in[q] = turned.T.astype(bf16)
+        cp = pltpu.make_async_copy(d_in.at[q], d_in_hbm.at[q], store_sem.at[PIECES + q])
+        cp.start()
+        stores.append(cp)
+
+    for j in range(2):
+        for k in range(1, experts):
+            plane_copy(grad_go.at[j], grad_came.at[j], grad_send.at[j], grad_recv.at[j], k).wait()
+        d_tok[j] = contract(pick_sel[...], grad_came[j], 0, 0).astype(bf16)
+        cp = pltpu.make_async_copy(
+            d_tok.at[j], d_tok_hbm.at[:, pl.ds(j * piece, piece)], store_sem.at[2 * PIECES + j]
+        )
+        cp.start()
+        stores.append(cp)
+
+    for k in range(1, 2 * planes):
+        gate_copy(k).wait()
+    total = gate_all[0]
+    for i in range(1, 2 * planes):
+        total += gate_all[i]
+    gate_total[...] = total
+
+    for a in range(2):
+        for j in range(2):
+            for t in range(planes):
+                twin_copy(a, j, t).wait_send()
+                if t < planes - 1:
+                    ring_up(a, j, t).wait_send()
+                    ring_down(a, j, t).wait_send()
+    for j in range(2):
+        for t in (planes - 2, planes - 1):
+            part_copy(j, t).wait_send()
+            sum_up(j, t).wait_send()
+            sum_down(j, t).wait_send()
+    for cp in stores:
+        cp.wait()
+
+
+def fast(cap, tokens, cotangent, w_in, w_out, pick_sel, pack_sel, gate_steps):
+    planes = lax.axis_size("patch")
+    experts = lax.axis_size("expert")
+    tok_dev, width = tokens.shape
+    units = w_in.shape[1]
+    piece = width // PIECES
+    pairs = experts * ROWS_PER_PAIR
+    vmem = pl.BlockSpec(memory_space=pltpu.VMEM)
+    hbm = pl.BlockSpec(memory_space=pl.ANY)
+    dma = pltpu.SemaphoreType.DMA
+    scratch = [
+        pltpu.VMEM((2, 2, tok_dev, piece), bf16),
+        pltpu.VMEM((2, 2, pairs, piece), bf16),
+        pltpu.VMEM((2, 2, pairs, piece), bf16),
+        pltpu.VMEM((2, PIECES, planes, cap, piece), bf16),
+        pltpu.VMEM((PIECES, piece, units), bf16),
+        pltpu.VMEM((units, width), bf16),
+        pltpu.VMEM((planes, cap, units), bf16),
+        pltpu.VMEM((planes, cap, units), bf16),
+        pltpu.VMEM((2, cap, piece), f32),
+        pltpu.VMEM((2, 2, cap, piece), bf16),
+        pltpu.VMEM((planes, 2, cap, piece), bf16),
+        pltpu.VMEM((2, 2, cap, piece), bf16),
+        pltpu.VMEM((planes, 2, cap, piece), bf16),
+        pltpu.VMEM((2, pairs, piece), bf16),
+        pltpu.VMEM((2, pairs, piece), bf16),
+        pltpu.VMEM((2, tok_dev, piece), bf16),
+        pltpu.VMEM((PIECES, piece, units), bf16),
+        pltpu.VMEM((PIECES, units, piece), bf16),
+        pltpu.VMEM((planes, 256), f32),
+        pltpu.VMEM((planes, 256), f32),
+        pltpu.VMEM((2 * planes, planes, 256), f32),
+        dma((6,)),
+        dma((2, 2, experts)),
+        dma((2, 2, experts)),
+        dma((2, 2, 2, planes)),
+        dma((2, 2, 2, planes)),
+        dma((2, 2, planes)),
+        dma((2, 2, planes)),
+        dma((planes, 2)),
+        dma((planes, 2)),
+        dma((2, 2, planes)),
+        dma((2, 2, planes)),
+        dma((2, experts)),
+        dma((2, experts)),
+        dma((2 * planes,)),
+        dma((2 * planes,)),
+        dma((2 * PIECES + 2,)),
+    ]
+    return pl.pallas_call(
+        functools.partial(kernel, planes, experts, cap),
+        out_shape=(
+            jax.ShapeDtypeStruct((tok_dev, width // 2), bf16),
+            jax.ShapeDtypeStruct((PIECES, piece, units), bf16),
+            jax.ShapeDtypeStruct((units, width), bf16),
+            jax.ShapeDtypeStruct((planes, 256), f32),
+        ),
+        in_specs=[hbm, hbm, hbm, hbm, vmem, vmem, vmem],
+        out_specs=(hbm, hbm, hbm, vmem),
+        scratch_shapes=scratch,
+        compiler_params=pltpu.CompilerParams(
+            collective_id=0, has_side_effects=True, vmem_limit_bytes=60 * 2**20
+        ),
+    )(
+        tokens,
+        cotangent,
+        w_in.reshape(PIECES, piece, units),
+        w_out,
+        pick_sel,
+        pack_sel,
+        gate_steps,
+    )
+
+
+def local(tokens, cotangent, w_in, w_out, gates, picks, counts):
+    tok_dev, width = tokens.shape
+    planes = lax.axis_size("patch")
+    experts = lax.axis_size("expert")
+    hidden_parts = lax.axis_size("hidden")
+    capacity = picks.shape[1]
+    sources = planes * experts
+    slots = capacity // planes
+    cap = 5 * slots // 4
+    half = cap // 2
+    z = lax.axis_index("patch")
+    e = lax.axis_index("expert")
+    c = lax.axis_index("hidden")
+    place = jnp.arange(capacity, dtype=jnp.int32)
+    codes = jnp.where(place[None, :] < counts[:, None], picks, -1)
+    plane_rows = tok_dev * experts
+    plane_ids = jnp.arange(planes, dtype=jnp.int32)
+    loads = jnp.sum(
+        (
+            (codes[:, :, None] >= plane_ids * plane_rows)
+            & (codes[:, :, None] < (plane_ids + 1) * plane_rows)
+        ).astype(jnp.int32),
+        axis=1,
+    )
+    fits = jnp.max(loads) <= cap
+
+    tok_ids = jnp.arange(tok_dev, dtype=jnp.int32)
+    source = z * experts + e
+    before = (tok_ids[:, None] < tok_ids[None, :]).astype(bf16)
+    taken = jnp.any(codes[:, :, None] == source * tok_dev + tok_ids, axis=1)
+    order = jnp.dot(taken.astype(bf16), before, preferred_element_type=f32).astype(jnp.int32)
+    pair_ids = jnp.arange(ROWS_PER_PAIR, dtype=jnp.int32)
+    pick_sel = (
+        (taken[:, None, :] & (order[:, None, :] == pair_ids[None, :, None]))
+        .astype(bf16)
+        .reshape(experts * ROWS_PER_PAIR, tok_dev)
+    )
+
+    mine = lax.dynamic_slice_in_dim(codes, e, 1, 0)[0]
+    holder = jnp.where(mine < 0, -1, mine // tok_dev)
+    row = mine % tok_dev
+    source_ids = jnp.arange(sources, dtype=jnp.int32)
+    by_holder = (holder[:, None] == source_ids).astype(bf16)
+    by_row = (row[:, None] == tok_ids).astype(bf16)
+    chosen = contract(by_holder, by_row, 0, 0)
+    ranks = jnp.dot(chosen.astype(bf16), before, preferred_element_type=f32)
+    sizes = jnp.sum(chosen, axis=1)
+    ahead = (source_ids[:, None] // experts == source_ids[None, :] // experts) & (
+        source_ids[None, :] < source_ids[:, None]
+    )
+    offsets = jnp.sum(jnp.where(ahead, sizes[None, :], 0.0), axis=1)
+    dest = (offsets[:, None] + ranks).astype(bf16)
+    spot = jnp.sum(
+        jnp.dot(by_holder, dest, preferred_element_type=f32) * by_row.astype(f32), axis=1
+    ).astype(jnp.int32)
+    block = holder // experts
+    my_sizes = lax.dynamic_slice_in_dim(sizes, z * experts, experts, 0).astype(jnp.int32)
+    my_offsets = lax.dynamic_slice_in_dim(offsets, z * experts, experts, 0).astype(jnp.int32)
+    target = jnp.where(
+        pair_ids[None, :] < my_sizes[:, None], my_offsets[:, None] + pair_ids[None, :], -1
+    ).reshape(-1)
+    pack_sel = (jnp.arange(cap, dtype=jnp.int32)[:, None] == target[None, :]).astype(bf16)
+    when = jnp.where(spot < half, (z - block + planes) % planes, (block - z + planes) % planes)
+    step_spot = jnp.where(mine < 0, -1, when * cap + spot)
+    gate_steps = jnp.sum(
+        jnp.where(
+            jnp.arange(planes * cap, dtype=jnp.int32)[:, None] == step_spot[None, :],
+            gates[0][None, :],
+            0.0,
+        ),
+        axis=1,
+    ).reshape(planes, cap, 1)
+    table_spot = jnp.where(mine < 0, -1, block * 256 + spot)
+    per_device = slots // hidden_parts
+    my_spot = lax.dynamic_slice_in_dim(
+        table_spot, (z * hidden_parts + c) * per_device, per_device, 0
+    )
+
+    def quick(tokens, cotangent, w_in, w_out, gates, picks, counts):
+        d_tokens, d_in, d_out, total = fast(
+            cap, tokens, cotangent, w_in[0], w_out[0], pick_sel, pack_sel, gate_steps
+        )
+        flat = total.reshape(-1)
+        found = my_spot[:, None] == jnp.arange(flat.shape[0], dtype=jnp.int32)[None, :]
+        d_gates = jnp.sum(jnp.where(found, flat[None, :], 0.0), axis=1)
+        return (d_tokens, d_in.reshape(w_in.shape), d_out[None], d_gates[None])
+
+    return lax.cond(fits, quick, general, tokens, cotangent, w_in, w_out, gates, picks, counts)
+
+
 def solution(mesh):
     in_specs = (
         P(("patch", "expert"), None),

time: 584 us -> 230 us (0.39)
  waiting for transfers between devices: 333 us -> 0 us
  Pallas kernels: 0 us -> 194 us
  local copies, waits for them, and re-layouts: 104 us -> 10.6 us
  blocking collectives: 42 us -> 0 us
  starting transfers between devices: 37 us -> 0 us
  matrix products: 35.5 us -> 1.01 us
  other arithmetic: 17 us -> 8.66 us
    pallas_call x0 -> x1, Pallas kernels: none -> 194 us  [fast(): pl.pallas_call(functools.partial(kernel, planes, experts, cap), out_shape...]
    all_gather x2 -> x0, waiting for transfers between devices: 179 us -> none  [the longest x1 90 us: local(): lax.all_gather(block_rows, 'patch', axis=0, tiled=True)]
    all_to_all x3 -> x0, waiting for transfers between devices: 84.4 us -> none  [the longest x1 46.1 us: local(): lax.all_to_all(send_grads, ('patch', 'expert'), split_axis=0, concat_axis...]
    reduce_scatter x1 -> x0, waiting for transfers between devices: 68.7 us -> none  [local(): lax.psum_scatter(slot_terms, ('patch', 'hidden'), scatter_dimension=0, ti...]
    scatter x2 -> x0, local copies, waits for them, and re-layouts: 62.5 us -> none  [the longest x1 60.3 us: local(): send_table = jnp.full((limit,), tok_dev, jnp.int32).at[position.reshape(-...]
    unnamed x1 -> x0, blocking collectives: 42 us -> none
    all_to_all x3 -> x0, starting transfers between devices: 36.7 us -> none  [the longest x1 15.9 us: local(): lax.all_to_all(send_grads, ('patch', 'expert'), split_axis=0, concat_axis...]
    dot_general x6 -> x3, matrix products: 35.5 us -> 1.01 us  [the longest x1 0.48 us: local(): jnp.dot(by_holder, dest, preferred_element_type=f32) * by_row.astype(f32)]
  transfers between devices with their start and end apart: 6 -> 0, of which waited for: 5 -> 0; matrix products, arithmetic and copies ran while one was open for 7% -> 0% of each run, Pallas kernels for 0% -> 0%
where the time goes in v1:
time: 230 us; the launch traced here: 229 us
  Pallas kernels  194 us (84%)
  between operations  14.9 us (6%)
  local copies, waits for them, and re-layouts  10.6 us (5%)
  other arithmetic  8.66 us (4%)
    pallas_call x1, Pallas kernels, fast(): pl.pallas_call(functools.partial(kernel, planes, experts, cap), out_shape...  194 us
    unnamed x17, local copies, waits for them, and re-layouts  5.35 us

profile of v1, /device:TPU:4, one launch (start us, length us, event | category | flops | bytes accessed | tf_op | source)
XLA Modules:
  0.0 229.4 jit_solution(13504372401199472053)
XLA Ops:
  7.2 0.1 eq.181
  7.3 0.9 fusion.52
  8.2 2.8 %compare_reduce_fusion = pred[16,128]{1,0:T(8,128)(4,1)S(1)} fusion(s32[128]{0:T(128)S(1)} %iota_add_fusion, s32[16,1024]{1,0:T(8,128)S(1)} %fusion.52), kind=kLoop, calls=%fused_computation.109 | loop fusion | flops 4192256 | bytes 68096 | tf_op jit(solution)/shard_map/reduce_or | solution.py:599
  11.0 0.4 convert_reduce_fusion.1
  11.4 0.6 reduce_max.9
  12.7 0.1 compare_select_fusion.15
  12.8 0.1 convolution_convert_fusion.3
  13.0 0.4 fusion.66
  13.4 0.2 select_reduce_fusion.2
  13.6 0.5 fusion.42
  14.1 0.1 dynamic-slice_convert_fusion
  14.2 0.1 add.273
  14.2 0.1 add.274
  14.3 0.1 lt.226
  14.4 0.1 lt.227
  14.5 0.1 fusion.51
  14.6 0.0 copy-start
  14.6 0.0 copy-start.1
  14.7 0.0 copy-start.5
  14.7 0.0 copy-start.6
  14.7 0.0 copy-start.7
  14.7 2.7 %eq.196 = s32[1280,1024]{1,0:T(8,128)} iota(), iota_dimension=0 | iota | bytes 5242880 | tf_op jit(solution)/shard_map/eq | solution.py:636
  17.4 0.0 copy-done
  17.5 0.0 copy-done.1
  17.5 0.0 copy-done.5
  17.5 0.0 copy-done.6
  17.5 0.0 copy-done.7
  17.5 199.7 %conditional.1 = (bf16[128,2048]{1,0:T(8,128)(2,1)S(1)}, bf16[1,4096,256]{2,1,0:T(8,128)(2,1)}, bf16[1,256,4096]{2,1,0:T(8,128)(2,1)}, f32[1,64]{1,0:T(1,128)S(1)}) conditional(s32[]{:T(128)} %convert_element_type.107, (s32[16,1024]{1,0:T(8,128)S(1)}, s32[16]{0:T(128)S(1)}, f32[1,1024]{1,0:T(1,128)S(1)}, bf16[128,4096]{1,0:T(8,128)(2,1)S(1)}, ...), branch_computations={%region_7.17_spmd, %region_15.19_spmd} | conditional | flops 10901746688 | bytes 223375088 | solution.py:657
  17.8 3.1 %select_reduce_fusion = f32[1280]{0:T(1024)S(1)} fusion(f32[]{:T(128)} %get-tuple-element.63, s32[1280,1024]{1,0:T(8,128)} %get-tuple-element.79, s32[1024]{0:T(1024)S(1)} %bitcast.120, f32[]{:T(128)} %get-tuple-element.82, f32[1024]{0:T(1024)S(1)} %bitcast.124), kind=kLoop, calls=%fused_computation.6 | loop fusion | flops 3930880 | bytes 5256200 | tf_op jit(solution)/shard_map/reduce_sum | solution.py:634
  20.9 0.1 dynamic_slice.27
  21.0 1.3 reshape.521.gate_ref
  22.3 194.0 %branch_1_fun.1 = (bf16[128,2048]{1,0:T(8,128)(2,1)S(1)}, bf16[4,1024,256]{2,1,0:T(8,128)(2,1)}, bf16[256,4096]{1,0:T(8,128)(2,1)}, f32[8,256]{1,0:T(8,128)}) custom-call(bf16[128,4096]{1,0:T(8,128)(2,1)S(1)} %get-tuple-element.39.tokens, bf16[128,4096]{1,0:T(8,128)(2,1)S(1)} %get-tuple-element.40.cotangent, bf16[4,1024,256]{2,1,0:T(8,128)(2,1)} %bitcast.104, ...), custom_call_target="tpu_custom_call" | custom-call | tf_op jit(solution)/shard_map/cond/branch_1_fun/pallas_call | solution.py:545
  216.3 0.7 copy.25
  217.0 0.2 select_reduce_fusion.1
  217.2 0.0 copy-start.9
  217.2 0.8 copy.40
  218.0 0.0 copy-start.4
  218.0 3.2 %copy.41 = bf16[1,4096,256]{2,1,0:T(8,128)(2,1)} copy(bf16[1,4096,256]{2,1,0:T(8,128)(2,1)} %get-tuple-element.183) | data formatting | bytes 4194304
  221.2 0.0 copy-done.9
  221.2 0.0 copy-done.4
  221.2 1.3 copy.42
  (19 shorter events, 0.2 us)
Async XLA Ops:
  14.6 2.8 %copy-start = (bf16[128,4096]{1,0:T(8,128)(2,1)S(1)}, bf16[128,4096]{1,0:T(8,128)(2,1)}, u32[]{:S(2)}) copy-start(bf16[128,4096]{1,0:T(8,128)(2,1)} %param.14) | copy-start | bytes 3145732
  14.6 2.8 %copy-start.1 = (bf16[128,4096]{1,0:T(8,128)(2,1)S(1)}, bf16[128,4096]{1,0:T(8,128)(2,1)}, u32[]{:S(2)}) copy-start(bf16[128,4096]{1,0:T(8,128)(2,1)} %param.13) | copy-start | bytes 3145732
  14.7 2.8 %copy-start.5 = (s32[16,1024]{1,0:T(8,128)S(1)}, s32[16,1024]{1,0:T(8,128)}, u32[]{:S(2)}) copy-start(s32[16,1024]{1,0:T(8,128)} %param.18) | copy-start | bytes 196612
  14.7 2.8 %copy-start.6 = (f32[1,1024]{1,0:T(1,128)S(1)}, f32[1,1024]{1,0:T(1,128)}, u32[]{:S(2)}) copy-start(f32[1,1024]{1,0:T(1,128)} %param.17) | copy-start | bytes 12292
  14.7 2.8 %copy-start.7 = (s32[16]{0:T(128)S(1)}, s32[16]{0:T(128)}, u32[]{:S(2)}) copy-start(s32[16]{0:T(128)} %param.19) | copy-start | bytes 196
  217.2 4.0 %copy-start.9 = (f32[1,64]{1,0:T(1,128)}, f32[1,64]{1,0:T(1,128)S(1)}, u32[]{:S(2)}) copy-start(f32[1,64]{1,0:T(1,128)S(1)} %get-tuple-element.185) | copy-start | bytes 772
  218.0 3.2 %copy-start.4 = (bf16[1,256,4096]{2,1,0:T(8,128)(2,1)S(1)}, bf16[1,256,4096]{2,1,0:T(8,128)(2,1)}, u32[]{:S(2)}) copy-start(bf16[1,256,4096]{2,1,0:T(8,128)(2,1)} %get-tuple-element.184) | copy-start | bytes 6291460

commit v2 on v1

v2 whole, which is shorter than its diff:
```python
import functools

import jax
import jax.numpy as jnp
from jax import lax
from jax.experimental import pallas as pl
from jax.experimental.pallas import tpu as pltpu
from jax.sharding import PartitionSpec as P

inv_root_two = 0.7071067811865476
inv_root_two_pi = 0.3989422804014327


def gelu_parts(pre):
    normal_cdf = 0.5 * (1.0 + lax.erf(pre * inv_root_two))
    density = jnp.exp(-0.5 * pre * pre) * inv_root_two_pi
    return (pre * normal_cdf, normal_cdf + pre * density)


def general(tokens, cotangent, w_in, w_out, gates, picks, counts):
    tok_dev, width = tokens.shape
    patch_count = lax.axis_size("patch")
    expert_count = lax.axis_size("expert")
    hidden_parts = lax.axis_size("hidden")
    capacity = picks.shape[1]
    slots = capacity // patch_count
    sources = patch_count * expert_count
    bound = 2 * max(1, slots // sources)
    limit = sources * bound
    patch_here = lax.axis_index("patch")
    expert_here = lax.axis_index("expert")
    source_here = patch_here * expert_count + expert_here
    slot_ids = jnp.arange(capacity, dtype=jnp.int32)
    live = slot_ids[None, :] < counts[:, None]
    holder = picks // tok_dev
    local_row = picks % tok_dev
    mine = (
        ((holder == source_here) & live).reshape(expert_count, patch_count, slots).astype(jnp.int32)
    )
    order_mine = jnp.cumsum(mine, axis=2) - 1
    expert_ids = jnp.arange(expert_count, dtype=jnp.int32)[:, None, None]
    patch_ids = jnp.arange(patch_count, dtype=jnp.int32)[None, :, None]
    position = (patch_ids * expert_count + expert_ids) * bound + order_mine
    position = jnp.where(mine == 1, position, limit)
    send_table = (
        jnp.full((limit,), tok_dev, jnp.int32)
        .at[position.reshape(-1)]
        .set(local_row.reshape(-1), mode="drop")
    )
    send_rows = jnp.take(tokens, send_table, axis=0, mode="fill", fill_value=0).reshape(
        sources, bound, width
    )
    send_grads = jnp.take(cotangent, send_table, axis=0, mode="fill", fill_value=0).reshape(
        sources, bound, width
    )
    came_rows, came_grads = (
        lax.all_to_all(send_rows, ("patch", "expert"), split_axis=0, concat_axis=0, tiled=True),
        lax.all_to_all(send_grads, ("patch", "expert"), split_axis=0, concat_axis=0, tiled=True),
    )
    my_picks = lax.dynamic_slice_in_dim(picks, expert_here, 1, 0)[0]
    block_picks = lax.dynamic_slice_in_dim(my_picks, patch_here * slots, slots, 0)
    count_here = lax.dynamic_slice_in_dim(counts, expert_here, 1, 0)[0]
    within = jnp.arange(slots, dtype=jnp.int32)
    block_live = patch_here * slots + within < count_here
    block_holder = block_picks // tok_dev
    earlier_same = (
        (block_holder[:, None] == block_holder[None, :])
        & block_live[None, :]
        & (within[None, :] < within[:, None])
    )
    block_order = jnp.sum(earlier_same.astype(jnp.int32), axis=1)
    came_index = jnp.where(block_live, block_holder * bound + block_order, limit)
    block_rows = jnp.take(
        came_rows.reshape(limit, width), came_index, axis=0, mode="fill", fill_value=0
    )
    block_grads = jnp.take(
        came_grads.reshape(limit, width), came_index, axis=0, mode="fill", fill_value=0
    )
    slot_rows, grad_rows = (
        lax.all_gather(block_rows, "patch", axis=0, tiled=True),
        lax.all_gather(block_grads, "patch", axis=0, tiled=True),
    )
    gate_col = gates[0][:, None]
    weight_in = w_in[0]
    weight_out = w_out[0]
    unit_count = weight_in.shape[1]
    pre = jnp.dot(slot_rows, weight_in, preferred_element_type=jnp.float32)
    act, slope = gelu_parts(pre)
    act_b = act.astype(jnp.bfloat16)
    back_act = lax.dot_general(
        grad_rows, weight_out, (((1,), (1,)), ((), ())), preferred_element_type=jnp.float32
    )
    gate_grad = jnp.sum(act * back_act, axis=1)
    back_pre = (gate_col * back_act * slope).astype(jnp.bfloat16)
    gated_rows = (gate_col * grad_rows.astype(jnp.float32)).astype(jnp.bfloat16)
    grad_in = lax.dot_general(
        slot_rows, back_pre, (((0,), (0,)), ((), ())), preferred_element_type=jnp.float32
    )
    grad_out = lax.dot_general(
        act_b, gated_rows, (((0,), (0,)), ((), ())), preferred_element_type=jnp.float32
    )
    gate_terms = gate_grad.reshape(patch_count * hidden_parts, slots // hidden_parts)
    d_gates = lax.psum_scatter(gate_terms, ("patch", "hidden"), scatter_dimension=0, tiled=True)
    selector = (jnp.arange(tok_dev, dtype=jnp.int32)[:, None] == send_table[None, :]).astype(
        jnp.bfloat16
    )
    back_blocks = back_pre.reshape(patch_count, slots, unit_count)
    weight_halves = weight_in.reshape(hidden_parts, width // hidden_parts, unit_count)
    slot_terms = jnp.einsum(
        "psf,hdf->phsd", back_blocks, weight_halves, preferred_element_type=jnp.float32
    ).astype(jnp.bfloat16)
    slot_terms = slot_terms.reshape(patch_count * hidden_parts, slots, width // hidden_parts)
    slot_sum = lax.psum_scatter(
        slot_terms, ("patch", "hidden"), scatter_dimension=0, tiled=True
    ).astype(jnp.float32)[0]
    slot_grad = slot_sum.astype(jnp.bfloat16)
    going_back = (
        jnp.zeros((limit, width // hidden_parts), jnp.bfloat16)
        .at[came_index]
        .set(slot_grad, mode="drop")
    )
    send_width = width // hidden_parts
    returned = lax.all_to_all(
        going_back.reshape(sources, bound, send_width),
        ("patch", "expert"),
        split_axis=0,
        concat_axis=0,
        tiled=True,
    )
    returned = returned.reshape(limit, send_width)
    token_grad = jnp.dot(selector, returned, preferred_element_type=jnp.float32)
    d_tokens = token_grad.astype(jnp.bfloat16)
    return (
        d_tokens,
        grad_in.astype(jnp.bfloat16)[None],
        grad_out.astype(jnp.bfloat16)[None],
        d_gates,
    )


MESH = pl.DeviceIdType.MESH
f32 = jnp.float32
bf16 = jnp.bfloat16
i32 = jnp.int32
PAIR = 16
PIECES = 4
CAP = 128
HALF = CAP // 2
SPILL = 32
FULL = 128


def contract(a, b, dim_a, dim_b):
    return lax.dot_general(a, b, (((dim_a,), (dim_b,)), ((), ())), preferred_element_type=f32)


def marks(mask):
    return jnp.where(mask, 1.0, 0.0).astype(bf16)


def iota(shape, dim):
    return lax.broadcasted_iota(i32, shape, dim)


def split_three(x):
    a = x.astype(bf16)
    rest = x - a.astype(f32)
    b = rest.astype(bf16)
    return (a, b, (rest - b.astype(f32)).astype(bf16))


def row_sums(x):
    ones = jnp.ones((8, x.shape[1]), bf16)
    return sum(contract(ones, part, 1, 1) for part in split_three(x))[0:1]


def previous(x):
    return pltpu.roll(x, 1, 0)


def following(x):
    return pltpu.roll(x, x.shape[0] - 1, 0)


def kernel(
    planes,
    experts,
    tokens,
    cotangent,
    w_in_hbm,
    w_out_hbm,
    gates,
    picks,
    counts,
    d_tok_hbm,
    d_in_hbm,
    d_out_hbm,
    d_gates,
    misfit,
    codes,
    taken,
    meta,
    tables,
    offs,
    lens,
    pick_sel,
    pack_sel,
    spill_sel,
    held,
    going,
    came,
    spilled,
    allrows,
    win,
    wout,
    act_s,
    back_s,
    home,
    part_out,
    part_in,
    sum_out,
    sum_in,
    grad_go,
    grad_came,
    grad_ret,
    d_tok,
    d_in,
    d_out,
    gate_lo,
    gate_hi,
    gate_all,
    load_sem,
    go_send,
    go_recv,
    spill_send,
    spill_recv,
    ring_send,
    ring_recv,
    twin_send,
    twin_recv,
    part_send,
    part_recv,
    sum_send,
    sum_recv,
    ret_send,
    ret_recv,
    grad_send,
    grad_recv,
    gate_send,
    gate_recv,
    store_sem,
):
    z = lax.axis_index("patch")
    e = lax.axis_index("expert")
    c = lax.axis_index("hidden")
    other = 1 - c
    up = (lax.rem(z + 1, planes), e, c)
    down = (lax.rem(z + planes - 1, planes), e, c)
    twin = (z, e, other)
    piece = held.shape[3]
    pairs = experts * PAIR
    capacity = codes.shape[1]
    plane_peers = [(z, lax.rem(e + k, experts), c) for k in range(1, experts)]
    me = z * 2 + c
    column_ids = [lax.rem(me + k, 2 * planes) for k in range(1, 2 * planes)]
    column_peers = [(i // 2, e, lax.rem(i, 2)) for i in column_ids]

    barrier = pltpu.get_barrier_semaphore()
    for peer in plane_peers + column_peers:
        pl.semaphore_signal(barrier, inc=1, device_id=peer, device_id_type=MESH)

    loads = []
    for a, ref in enumerate((tokens, cotangent)):
        for j in range(2):
            col = pl.multiple_of((2 * c + j) * piece, piece)
            cp = pltpu.make_async_copy(
                ref.at[:, pl.ds(col, piece)], held.at[a, j], load_sem.at[2 * a + j]
            )
            cp.start()
            loads.append(cp)
    load_in = pltpu.make_async_copy(w_in_hbm, win, load_sem.at[4])
    load_out = pltpu.make_async_copy(w_out_hbm, wout, load_sem.at[5])
    load_in.start()
    load_out.start()

    before = marks(iota((FULL, FULL), 0) < iota((FULL, FULL), 1))
    place = iota((1, capacity), 1)
    for i in range(experts):
        codes[i : i + 1, :] = jnp.where(place < counts[i], picks[i : i + 1, :], -1)
    base = (z * experts + e) * FULL
    wanted = iota((FULL, capacity), 0) + base

    def find(i, carry):
        match = jnp.where(codes[pl.ds(i, 1), :] == wanted, 1.0, 0.0)
        folded = match[:, 0:FULL]
        for k in range(1, capacity // FULL):
            folded += match[:, k * FULL : (k + 1) * FULL]
        taken[pl.ds(i, 1), :] = contract(jnp.ones((8, FULL), bf16), folded.astype(bf16), 1, 1)[0:1]
        return carry

    lax.fori_loop(0, experts, find, 0)
    present = taken[...]
    order = contract(present.astype(bf16), before, 1, 0)
    order = jnp.where(present > 0.5, order, -1.0).astype(i32)
    for i in range(experts):
        pick_sel[i * PAIR : (i + 1) * PAIR, :] = marks(
            iota((PAIR, FULL), 0) == order[i : i + 1, :]
        )

    pl.semaphore_wait(barrier, len(plane_peers) + len(column_peers))

    def remote(src, dst, s, r, dev):
        return pltpu.make_async_remote_copy(
            src_ref=src, dst_ref=dst, send_sem=s, recv_sem=r, device_id=dev, device_id_type=MESH
        )

    own_rows = pl.ds(pl.multiple_of(e * PAIR, PAIR), PAIR)

    def plane_copy(src, dst, ssem, rsem, k):
        to = pl.multiple_of(lax.rem(e + k, experts) * PAIR, PAIR)
        return remote(
            src.at[pl.ds(to, PAIR)], dst.at[own_rows], ssem.at[k], rsem.at[k], plane_peers[k - 1]
        )

    def go_copy(a, j, k):
        return plane_copy(
            going.at[a, j], came.at[a, j], go_send.at[a, j], go_recv.at[a, j], k
        )

    def grad_copy(j, k):
        return plane_copy(
            grad_go.at[j], grad_came.at[j], grad_send.at[j], grad_recv.at[j], k
        )

    def spill_up(a, j):
        return remote(
            spilled.at[a, j, pl.ds(0, SPILL)],
            came.at[a, j, pl.ds(pairs, SPILL)],
            spill_send.at[0, a, j],
            spill_recv.at[0, a, j],
            up,
        )

    def spill_down(a, j):
        return remote(
            spilled.at[a, j, pl.ds(SPILL, SPILL)],
            came.at[a, j, pl.ds(pairs + SPILL, SPILL)],
            spill_send.at[1, a, j],
            spill_recv.at[1, a, j],
            down,
        )

    def ret_down(j):
        return remote(
            grad_go.at[j, pl.ds(pairs, SPILL)],
            grad_ret.at[j, pl.ds(0, SPILL)],
            ret_send.at[0, j],
            ret_recv.at[0, j],
            down,
        )

    def ret_up(j):
        return remote(
            grad_go.at[j, pl.ds(pairs + SPILL, SPILL)],
            grad_ret.at[j, pl.ds(SPILL, SPILL)],
            ret_send.at[1, j],
            ret_recv.at[1, j],
            up,
        )

    def ring_up(a, j, t):
        q = 2 * c + j
        return remote(
            allrows.at[a, q, t, pl.ds(0, HALF)],
            allrows.at[a, q, t + 1, pl.ds(0, HALF)],
            ring_send.at[0, a, j, t],
            ring_recv.at[0, a, j, t + 1],
            up,
        )

    def ring_down(a, j, t):
        q = 2 * c + j
        return remote(
            allrows.at[a, q, t, pl.ds(HALF, HALF)],
            allrows.at[a, q, t + 1, pl.ds(HALF, HALF)],
            ring_send.at[1, a, j, t],
            ring_recv.at[1, a, j, t + 1],
            down,
        )

    def twin_copy(a, j, t):
        q = 2 * c + j
        return remote(
            allrows.at[a, q, t],
            allrows.at[a, q, t],
            twin_send.at[a, j, t],
            twin_recv.at[a, j, t],
            twin,
        )

    def part_copy(j, t):
        slot = lax.rem(t, 2)
        return remote(
            part_out.at[slot, j], part_in.at[t, j], part_send.at[t, j], part_recv.at[t, j], twin
        )

    def sum_up(j, t):
        return remote(
            sum_out.at[lax.rem(t, 2), j, pl.ds(0, HALF)],
            sum_in.at[t, j, pl.ds(0, HALF)],
            sum_send.at[0, j, t],
            sum_recv.at[0, j, t],
            up,
        )

    def sum_down(j, t):
        return remote(
            sum_out.at[lax.rem(t, 2), j, pl.ds(HALF, HALF)],
            sum_in.at[t, j, pl.ds(HALF, HALF)],
            sum_send.at[1, j, t],
            sum_recv.at[1, j, t],
            down,
        )

    for a in range(2):
        for j in range(2):
            loads[2 * a + j].wait()
            going[a, j] = contract(pick_sel[...], held[a, j], 1, 0).astype(bf16)
            came[a, j, own_rows, :] = going[a, j, own_rows, :]
            for k in range(1, experts):
                go_copy(a, j, k).start()

    mine = codes[pl.ds(e, 1), :]
    by_holder = marks((mine >> 7) == iota((FULL, capacity), 0))
    by_row = marks((mine & (FULL - 1)) == iota((FULL, capacity), 0))
    chosen = contract(by_holder, by_row, 1, 1).astype(bf16)
    ranks = contract(chosen, before, 1, 0)
    sizes = contract(chosen, jnp.ones((FULL, FULL), bf16), 1, 0)
    sizes_b = sizes.astype(bf16)
    from_s = iota((FULL, FULL), 1)
    to_s = iota((FULL, FULL), 0)
    ahead = marks((from_s // PAIR == to_s // PAIR) & (from_s < to_s))
    offsets = contract(ahead, sizes_b, 1, 0)
    offs[...] = offsets
    lens[...] = sizes
    group_lane = iota((planes, FULL), 1) // PAIR
    group_row = iota((planes, FULL), 0)
    grouped = marks(group_lane == group_row)
    amount = contract(grouped, sizes_b, 1, 0).astype(i32)
    so_far = contract(marks(group_lane <= group_row), sizes_b, 1, 0).astype(i32)
    live = so_far[planes - 1 : planes, :]
    excess = so_far - ((live * (group_row + 1)) >> 3)
    middle = (jnp.max(excess, axis=0, keepdims=True) + jnp.min(excess, axis=0, keepdims=True)) >> 1
    flow = excess - middle
    rising = jnp.maximum(flow, 0)
    sinking = jnp.maximum(-flow, 0)
    risen = previous(rising)
    keep = amount - rising - previous(sinking)
    up_at = following(keep)
    down_at = previous(keep + risen)
    for i, table in enumerate((keep, rising, risen, sinking)):
        tables[i] = table

    def spread(x):
        return contract(grouped, x.astype(bf16), 0, 0)

    keep_s, rising_s = spread(keep), spread(rising)
    dest = offsets + ranks - keep_s
    goes_up = (dest >= 0) & (dest < rising_s)
    goes_down = dest >= rising_s
    spot = jnp.where(
        dest < 0, dest + keep_s, jnp.where(goes_up, spread(up_at) + dest, spread(down_at) + dest - rising_s)
    )
    goes_down = (dest >= 0) & goes_down
    shift = jnp.where(goes_up, 1.0, jnp.where(goes_down, -1.0, 0.0))

    def per_slot(x):
        return jnp.sum(
            contract(x.astype(bf16), by_holder, 0, 0) * by_row.astype(f32), axis=0, keepdims=True
        ).astype(i32)

    slot = per_slot(spot)
    block = ((mine >> 11) + per_slot(shift)) & (planes - 1)
    when = jnp.where(slot < HALF, z - block, block - z) & (planes - 1)
    meta[0:1, :] = jnp.where(mine < 0, -1, when * CAP + slot)
    meta[1:2, :] = block
    meta[2:3, :] = jnp.where(mine < 0, -1, slot)

    own_group = pl.ds(pl.multiple_of(z * PAIR, PAIR), PAIR)
    widen = marks(iota((PAIR, pairs), 1) // PAIR == iota((PAIR, pairs), 0))
    start = contract(offs[own_group, :].astype(bf16), widen, 0, 0).astype(i32)
    size = contract(lens[own_group, :].astype(bf16), widen, 0, 0).astype(i32)
    index = iota((CAP, pairs), 1) & (PAIR - 1)
    spot_here = jnp.where(index < size, start + index, -1)

    def own(i):
        return tables[i, pl.ds(z, 1), :][:, 0:1]

    keep_z, rising_z, risen_z, sinking_z = own(0), own(1), own(2), own(3)
    line = iota((CAP, pairs), 0)
    pack_sel[:, 0:pairs] = marks((spot_here == line) & (line < keep_z))
    lane = iota((CAP, FULL), 1)
    line = iota((CAP, FULL), 0) - keep_z
    pack_sel[:, pairs : pairs + FULL] = marks(
        ((lane < SPILL) & (lane < risen_z) & (line == lane))
        | ((lane >= SPILL) & (lane < SPILL + sinking_z) & (line - risen_z == lane - SPILL))
    )
    line = iota((2 * SPILL, pairs), 0)
    above = spot_here[0 : 2 * SPILL, :] - keep_z
    spill_sel[...] = marks(
        ((line < SPILL) & (line < rising_z) & (above == line))
        | ((line >= SPILL) & (above - rising_z == line - SPILL) & (spot_here[0 : 2 * SPILL, :] >= 0))
    )

    all_codes = codes[...] >> 11
    held_by = [
        jnp.sum(jnp.where(all_codes == i, 1, 0), axis=1, keepdims=True) for i in range(planes)
    ]
    running = [held_by[0]]
    for i in range(1, planes):
        running.append(running[-1] + held_by[i])
    over = [running[i] - ((running[-1] * (i + 1)) >> 3) for i in range(planes)]
    most, least = over[0], over[0]
    for x in over[1:]:
        most, least = jnp.maximum(most, x), jnp.minimum(least, x)
    mid = (most + least) >> 1
    bad = jnp.maximum(most - mid, mid - least) - SPILL
    for i in range(planes):
        leaves = jnp.maximum(over[i] - mid, 0) + jnp.maximum(mid - over[i - 1], 0)
        bad = jnp.maximum(bad, leaves - held_by[i])
    misfit[...] = jnp.broadcast_to(jnp.max(bad, axis=0, keepdims=True), misfit.shape)

    for a in range(2):
        for j in range(2):
            came[a, j, pairs + 2 * SPILL :, :] = jnp.zeros((FULL - 2 * SPILL, piece), bf16)
    for a in range(2):
        for j in range(2):
            for k in range(1, experts):
                go_copy(a, j, k).wait()
            spilled[a, j] = contract(spill_sel[...], came[a, j, 0:pairs, :], 1, 0).astype(bf16)
            spill_up(a, j).start()
            spill_down(a, j).start()
            spill_up(a, j).wait()
            spill_down(a, j).wait()
            allrows[a, 2 * c + j, 0] = contract(pack_sel[...], came[a, j], 1, 0).astype(bf16)
            ring_up(a, j, 0).start()
            ring_down(a, j, 0).start()
            twin_copy(a, j, 0).start()
    load_in.wait()
    load_out.wait()

    def step(t, carry):
        for a in range(2):
            for j in range(2):

                @pl.when(t > 0)
                def _():
                    ring_up(a, j, t - 1).wait_recv()

                    @pl.when(t < planes - 1)
                    def _():
                        ring_up(a, j, t).start()

                    ring_down(a, j, t - 1).wait_recv()

                    @pl.when(t < planes - 1)
                    def _():
                        ring_down(a, j, t).start()

                    twin_copy(a, j, t).start()

        for a in range(2):
            for j in range(2):
                twin_copy(a, j, t).wait_recv()
        pre = contract(allrows[0, 0, t], win[0], 1, 0)
        back = contract(allrows[1, 0, t], wout[:, 0:piece], 1, 1)
        for q in range(1, PIECES):
            pre += contract(allrows[0, q, t], win[q], 1, 0)
            back += contract(allrows[1, q, t], wout[:, q * piece : (q + 1) * piece], 1, 1)
        act, slope = gelu_parts(pre)
        gate = jnp.sum(
            jnp.where(meta[0:1, :] == iota((CAP, capacity), 0) + t * CAP, gates[...], 0.0),
            axis=1,
            keepdims=True,
        )
        act_s[t] = (gate * act).astype(bf16)
        back_pre = (gate * back * slope).astype(bf16)
        back_s[t] = back_pre
        gate_row = row_sums(act * back)
        gate_lo[pl.ds(lax.rem(z + planes - t, planes), 1), :] = gate_row
        gate_hi[pl.ds(lax.rem(z + t, planes), 1), :] = gate_row

        for j in range(2):

            @pl.when(t > 1)
            def _():
                part_copy(j, t - 2).wait_send()

            part_out[lax.rem(t, 2), j] = contract(back_pre, win[2 * other + j], 1, 1).astype(bf16)
            part_copy(j, t).start()
        for j in range(2):
            own_part = contract(back_pre, win[2 * c + j], 1, 1)
            part_copy(j, t).wait_recv()
            own_part += part_in[t, j].astype(f32)

            @pl.when(t == 0)
            def _():
                home[j] = own_part

            @pl.when(t > 2)
            def _():
                sum_up(j, t - 2).wait_send()
                sum_down(j, t - 2).wait_send()

            @pl.when(t > 1)
            def _():
                sum_up(j, t - 1).wait_recv()
                sum_down(j, t - 1).wait_recv()
                sum_out[lax.rem(t, 2), j] = (own_part + sum_in[t - 1, j].astype(f32)).astype(bf16)

            @pl.when(t == 1)
            def _():
                sum_out[lax.rem(t, 2), j] = own_part.astype(bf16)

            @pl.when(t > 0)
            def _():
                sum_up(j, t).start()
                sum_down(j, t).start()

        return carry

    lax.fori_loop(0, planes, step, 0)

    gate_all[me] = jnp.where(iota(gate_lo.shape, 1) < HALF, gate_lo[...], gate_hi[...])

    def gate_copy(k):
        return remote(
            gate_all.at[me], gate_all.at[me], gate_send.at[k], gate_recv.at[k], column_peers[k - 1]
        )

    for k in range(1, 2 * planes):
        gate_copy(k).start()

    rows = planes * CAP
    act_all = act_s[...].reshape(rows, act_s.shape[2])
    for q in range(PIECES):
        d_out[q] = contract(act_all, allrows[1, q].reshape(rows, piece), 0, 0).astype(bf16)

    last = planes - 1
    for j in range(2):
        sum_up(j, last).wait_recv()
        sum_down(j, last).wait_recv()
        slot_grad = (home[j] + sum_in[last, j].astype(f32)).astype(bf16)
        grad_go[j, pairs:, :] = contract(pack_sel[:, pairs:], slot_grad, 0, 0).astype(bf16)
        ret_up(j).start()
        ret_down(j).start()
        grad_go[j, 0:pairs, :] = contract(pack_sel[:, 0:pairs], slot_grad, 0, 0).astype(bf16)
        ret_up(j).wait()
        ret_down(j).wait()
        returned = contract(spill_sel[...], grad_ret[j], 0, 0)
        grad_go[j, 0:pairs, :] = (grad_go[j, 0:pairs, :].astype(f32) + returned).astype(bf16)
        grad_came[j, own_rows, :] = grad_go[j, own_rows, :]
        for k in range(1, experts):
            grad_copy(j, k).start()

    stores = []
    for q in range(PIECES):
        cp = pltpu.make_async_copy(
            d_out.at[q], d_out_hbm.at[:, pl.ds(q * piece, piece)], store_sem.at[q]
        )
        cp.start()
        stores.append(cp)
    back_all = back_s[...].reshape(rows, back_s.shape[2])
    for q in range(PIECES):
        turned = contract(back_all, allrows[0, q].reshape(rows, piece), 0, 0)
        d_in[q] = turned.T.astype(bf16)
        cp = pltpu.make_async_copy(d_in.at[q], d_in_hbm.at[q], store_sem.at[PIECES + q])
        cp.start()
        stores.append(cp)

    for k in range(1, 2 * planes):
        gate_copy(k).wait()
    total = gate_all[0]
    for i in range(1, 2 * planes):
        total += gate_all[i]
    own_lanes = pl.ds(pl.multiple_of(z * CAP, CAP), CAP)
    found = marks(meta[2:3, own_lanes] == iota((CAP, CAP), 0))
    values = sum(contract(part, found, 1, 0) for part in split_three(total))
    values = jnp.sum(
        jnp.where(meta[1:2, own_lanes] == iota(values.shape, 0), values, 0.0),
        axis=0,
        keepdims=True,
    )
    d_gates[...] = jnp.where(c == 0, values[:, 0:HALF], values[:, HALF:])

    for j in range(2):
        for k in range(1, experts):
            grad_copy(j, k).wait()
        d_tok[j] = contract(pick_sel[...], grad_came[j], 0, 0).astype(bf16)
        cp = pltpu.make_async_copy(
            d_tok.at[j], d_tok_hbm.at[:, pl.ds(j * piece, piece)], store_sem.at[2 * PIECES + j]
        )
        cp.start()
        stores.append(cp)

    for a in range(2):
        for j in range(2):
            for t in range(planes):
                twin_copy(a, j, t).wait_send()
                if t < planes - 1:
                    ring_up(a, j, t).wait_send()
                    ring_down(a, j, t).wait_send()
    for j in range(2):
        for t in (planes - 2, planes - 1):
            part_copy(j, t).wait_send()
            sum_up(j, t).wait_send()
            sum_down(j, t).wait_send()
    for cp in stores:
        cp.wait()


def fast(tokens, cotangent, w_in, w_out, gates, picks, counts):
    planes = lax.axis_size("patch")
    experts = lax.axis_size("expert")
    tok_dev, width = tokens.shape
    units = w_in.shape[2]
    capacity = picks.shape[1]
    piece = width // PIECES
    pairs = experts * PAIR
    vmem = pl.BlockSpec(memory_space=pltpu.VMEM)
    smem = pl.BlockSpec(memory_space=pltpu.SMEM)
    hbm = pl.BlockSpec(memory_space=pl.ANY)
    dma = pltpu.SemaphoreType.DMA
    scratch = [
        pltpu.VMEM((experts, capacity), i32),
        pltpu.VMEM((experts, tok_dev), f32),
        pltpu.VMEM((8, capacity), i32),
        pltpu.VMEM((4, planes, FULL), i32),
        pltpu.VMEM((FULL, FULL), f32),
        pltpu.VMEM((FULL, FULL), f32),
        pltpu.VMEM((pairs, tok_dev), bf16),
        pltpu.VMEM((CAP, pairs + FULL), bf16),
        pltpu.VMEM((2 * SPILL, pairs), bf16),
        pltpu.VMEM((2, 2, tok_dev, piece), bf16),
        pltpu.VMEM((2, 2, pairs, piece), bf16),
        pltpu.VMEM((2, 2, pairs + FULL, piece), bf16),
        pltpu.VMEM((2, 2, 2 * SPILL, piece), bf16),
        pltpu.VMEM((2, PIECES, planes, CAP, piece), bf16),
        pltpu.VMEM((PIECES, piece, units), bf16),
        pltpu.VMEM((units, width), bf16),
        pltpu.VMEM((planes, CAP, units), bf16),
        pltpu.VMEM((planes, CAP, units), bf16),
        pltpu.VMEM((2, CAP, piece), f32),
        pltpu.VMEM((2, 2, CAP, piece), bf16),
        pltpu.VMEM((planes, 2, CAP, piece), bf16),
        pltpu.VMEM((2, 2, CAP, piece), bf16),
        pltpu.VMEM((planes, 2, CAP, piece), bf16),
        pltpu.VMEM((2, pairs + FULL, piece), bf16),
        pltpu.VMEM((2, pairs, piece), bf16),
        pltpu.VMEM((2, 2 * SPILL, piece), bf16),
        pltpu.VMEM((2, tok_dev, piece), bf16),
        pltpu.VMEM((PIECES, piece, units), bf16),
        pltpu.VMEM((PIECES, units, piece), bf16),
        pltpu.VMEM((planes, CAP), f32),
        pltpu.VMEM((planes, CAP), f32),
        pltpu.VMEM((2 * planes, planes, CAP), f32),
        dma((6,)),
        dma((2, 2, experts)),
        dma((2, 2, experts)),
        dma((2, 2, 2)),
        dma((2, 2, 2)),
        dma((2, 2, 2, planes)),
        dma((2, 2, 2, planes)),
        dma((2, 2, planes)),
        dma((2, 2, planes)),
        dma((planes, 2)),
        dma((planes, 2)),
        dma((2, 2, planes)),
        dma((2, 2, planes)),
        dma((2, 2)),
        dma((2, 2)),
        dma((2, experts)),
        dma((2, experts)),
        dma((2 * planes,)),
        dma((2 * planes,)),
        dma((2 * PIECES + 2,)),
    ]
    d_tokens, d_in, d_out, d_gates, misfit = pl.pallas_call(
        functools.partial(kernel, planes, experts),
        out_shape=(
            jax.ShapeDtypeStruct((tok_dev, width // 2), bf16),
            jax.ShapeDtypeStruct((PIECES, piece, units), bf16),
            jax.ShapeDtypeStruct((units, width), bf16),
            jax.ShapeDtypeStruct((1, HALF), f32),
            jax.ShapeDtypeStruct((8, FULL), i32),
        ),
        in_specs=[hbm, hbm, hbm, hbm, vmem, vmem, smem],
        out_specs=(hbm, hbm, hbm, vmem, vmem),
        scratch_shapes=scratch,
        compiler_params=pltpu.CompilerParams(
            collective_id=0, has_side_effects=True, vmem_limit_bytes=60 * 2**20
        ),
    )(tokens, cotangent, w_in.reshape(PIECES, piece, units), w_out[0], gates, picks, counts)
    return (d_tokens, d_in.reshape(w_in.shape), d_out[None], d_gates, misfit)


def local(*args):
    results = fast(*args)
    return lax.cond(
        results[4][0, 0] <= 0, lambda found, args: found, lambda found, args: general(*args), results[:4], args
    )


def solution(mesh):
    in_specs = (
        P(("patch", "expert"), None),
        P(("patch", "expert"), None),
        P("expert", None, ("patch", "hidden")),
        P("expert", ("patch", "hidden"), None),
        P("expert", None),
        P(),
        P(),
    )
    out_specs = (
        P(("patch", "expert"), "hidden"),
        P("expert", None, ("patch", "hidden")),
        P("expert", ("patch", "hidden"), None),
        P("expert", ("patch", "hidden")),
    )
    return jax.shard_map(local, mesh=mesh, in_specs=in_specs, out_specs=out_specs, check_vma=False)
```

time: 230 us -> 209 us (0.909)
  other arithmetic: 8.66 us -> 0 us
  Pallas kernels: 194 us -> 186 us
  local copies, waits for them, and re-layouts: 10.6 us -> 8.12 us
    pallas_call x1, Pallas kernels: 194 us -> 186 us  [fast(): pl.pallas_call(functools.partial(kernel, planes, experts), out_shape=(jax...]
    reduce_sum x4 -> x0, other arithmetic: 3.91 us -> none  [the longest x1 3.08 us: local(): jnp.sum(jnp.where(jnp.arange(planes * cap, dtype=jnp.int32)[:, None] == s...]
    eq x3 -> x0, local copies, waits for them, and re-layouts: 2.81 us -> none  [the longest x1 2.73 us: local(): jnp.arange(planes * cap, dtype=jnp.int32)[:, None] == step_spot[None, :]]
    reduce_or x1 -> x0, other arithmetic: 2.79 us -> none  [local(): taken = jnp.any(codes[:, :, None] == source * tok_dev + tok_ids, axis=1)]
    unnamed x17 -> x16, local copies, waits for them, and re-layouts: 5.35 us -> 6.93 us
where the time goes in v2:
time: 209 us
  Pallas kernels  186 us (89%)
  between operations  14.8 us (7%)
  local copies, waits for them, and re-layouts  8.12 us (4%)
    pallas_call x1, Pallas kernels, fast(): pl.pallas_call(functools.partial(kernel, planes, experts), out_shape=(jax...  186 us
    unnamed x16, local copies, waits for them, and re-layouts  6.93 us

profile of v2, /device:TPU:4, one launch (start us, length us, event | category | flops | bytes accessed | tf_op | source)
XLA Modules:
  0.0 209.2 jit_solution(6690877509115771201)
XLA Ops:
  7.2 0.0 copy-start
  7.2 0.0 copy-start.1
  7.2 0.0 copy-start.6
  7.2 0.0 copy-start.7
  7.2 0.0 copy-start.8
  7.2 186.0 %shard_map.110 = (bf16[128,2048]{1,0:T(8,128)(2,1)}, bf16[4,1024,256]{2,1,0:T(8,128)(2,1)}, bf16[256,4096]{1,0:T(8,128)(2,1)}, f32[1,64]{1,0:T(1,128)S(1)}, s32[8,128]{1,0:T(8,128)}) custom-call(bf16[128,4096]{1,0:T(8,128)(2,1)} %tokens.1, bf16[128,4096]{1,0:T(8,128)(2,1)} %cotangent.1, bf16[4,1024,256]{2,1,0:T(8,128)(2,1)} %bitcast.85, ...), custom_call_target="tpu_custom_call" | custom-call | tf_op jit(solution)/shard_map/pallas_call | solution.py:788
  193.3 1.2 slice.3
  195.1 0.0 copy-done
  195.1 0.0 copy-done.1
  195.1 0.0 copy-done.6
  195.1 0.0 copy-done.7
  195.2 0.0 copy-done.8
  195.2 0.2 conditional.1
  195.4 1.9 copy.35
  197.3 0.0 copy-start.5
  197.3 3.2 %copy.36 = bf16[1,4096,256]{2,1,0:T(8,128)(2,1)} copy(bf16[1,4096,256]{2,1,0:T(8,128)(2,1)} %get-tuple-element.88) | data formatting | bytes 4194304
  200.5 0.0 copy-done.5
  200.5 1.3 copy.37
  201.8 0.5 copy.38
Async XLA Ops:
  7.2 188.0 %copy-start = (bf16[128,4096]{1,0:T(8,128)(2,1)S(1)}, bf16[128,4096]{1,0:T(8,128)(2,1)}, u32[]{:S(2)}) copy-start(bf16[128,4096]{1,0:T(8,128)(2,1)} %tokens.1) | copy-start | bytes 3145732
  7.2 188.0 %copy-start.1 = (bf16[128,4096]{1,0:T(8,128)(2,1)S(1)}, bf16[128,4096]{1,0:T(8,128)(2,1)}, u32[]{:S(2)}) copy-start(bf16[128,4096]{1,0:T(8,128)(2,1)} %cotangent.1) | copy-start | bytes 3145732
  7.2 188.0 %copy-start.6 = (s32[16,1024]{1,0:T(8,128)S(1)}, s32[16,1024]{1,0:T(8,128)}, u32[]{:S(2)}) copy-start(s32[16,1024]{1,0:T(8,128)} %picks.1) | copy-start | bytes 196612
  7.2 188.0 %copy-start.7 = (f32[1,1024]{1,0:T(1,128)S(1)}, f32[1,1024]{1,0:T(1,128)}, u32[]{:S(2)}) copy-start(f32[1,1024]{1,0:T(1,128)} %gates.1) | copy-start | bytes 12292
  7.2 188.0 %copy-start.8 = (s32[16]{0:T(128)S(1)}, s32[16]{0:T(128)}, u32[]{:S(2)}) copy-start(s32[16]{0:T(128)} %counts.1) | copy-start | bytes 196
  197.3 3.2 %copy-start.5 = (bf16[1,256,4096]{2,1,0:T(8,128)(2,1)S(1)}, bf16[1,256,4096]{2,1,0:T(8,128)(2,1)}, u32[]{:S(2)}) copy-start(bf16[1,256,4096]{2,1,0:T(8,128)(2,1)} %get-tuple-element.89) | copy-start | bytes 6291460

commit v3 on v2

--- a/solution.py
+++ b/solution.py
@@ -430,6 +430,25 @@
             for k in range(1, experts):
                 go_copy(a, j, k).start()
 
+    def forward(p, t):
+        a, j = p // 2, p % 2
+
+        @pl.when(t < planes)
+        def _():
+            ring_up(a, j, t - 1).wait_recv()
+
+            @pl.when(t < planes - 1)
+            def _():
+                ring_up(a, j, t).start()
+
+            ring_down(a, j, t - 1).wait_recv()
+
+            @pl.when(t < planes - 1)
+            def _():
+                ring_down(a, j, t).start()
+
+            twin_copy(a, j, t).start()
+
     mine = codes[pl.ds(e, 1), :]
     by_holder = marks((mine >> 7) == iota((FULL, capacity), 0))
     by_row = marks((mine & (FULL - 1)) == iota((FULL, capacity), 0))
@@ -528,7 +547,7 @@
     for i in range(planes):
         leaves = jnp.maximum(over[i] - mid, 0) + jnp.maximum(mid - over[i - 1], 0)
         bad = jnp.maximum(bad, leaves - held_by[i])
-    misfit[...] = jnp.broadcast_to(jnp.max(bad, axis=0, keepdims=True), misfit.shape)
+    misfit[0] = jnp.max(bad)
 
     for a in range(2):
         for j in range(2):
@@ -540,6 +559,8 @@
             spilled[a, j] = contract(spill_sel[...], came[a, j, 0:pairs, :], 1, 0).astype(bf16)
             spill_up(a, j).start()
             spill_down(a, j).start()
+            for p in range(2 * a + j):
+                forward(p, 2 * a + j - p)
             spill_up(a, j).wait()
             spill_down(a, j).wait()
             allrows[a, 2 * c + j, 0] = contract(pack_sel[...], came[a, j], 1, 0).astype(bf16)
@@ -550,33 +571,16 @@
     load_out.wait()
 
     def step(t, carry):
-        for a in range(2):
-            for j in range(2):
-
-                @pl.when(t > 0)
-                def _():
-                    ring_up(a, j, t - 1).wait_recv()
-
-                    @pl.when(t < planes - 1)
-                    def _():
-                        ring_up(a, j, t).start()
-
-                    ring_down(a, j, t - 1).wait_recv()
-
-                    @pl.when(t < planes - 1)
-                    def _():
-                        ring_down(a, j, t).start()
-
-                    twin_copy(a, j, t).start()
-
-        for a in range(2):
-            for j in range(2):
-                twin_copy(a, j, t).wait_recv()
+        @pl.when(t > 0)
+        def _():
+            for p in range(3):
+                forward(p, t + 3 - p)
+
+        for j in range(2):
+            twin_copy(0, j, t).wait_recv()
         pre = contract(allrows[0, 0, t], win[0], 1, 0)
-        back = contract(allrows[1, 0, t], wout[:, 0:piece], 1, 1)
         for q in range(1, PIECES):
             pre += contract(allrows[0, q, t], win[q], 1, 0)
-            back += contract(allrows[1, q, t], wout[:, q * piece : (q + 1) * piece], 1, 1)
         act, slope = gelu_parts(pre)
         gate = jnp.sum(
             jnp.where(meta[0:1, :] == iota((CAP, capacity), 0) + t * CAP, gates[...], 0.0),
@@ -584,6 +588,16 @@
             keepdims=True,
         )
         act_s[t] = (gate * act).astype(bf16)
+
+        @pl.when(t > 0)
+        def _():
+            forward(3, t)
+
+        for j in range(2):
+            twin_copy(1, j, t).wait_recv()
+        back = contract(allrows[1, 0, t], wout[:, 0:piece], 1, 1)
+        for q in range(1, PIECES):
+            back += contract(allrows[1, q, t], wout[:, q * piece : (q + 1) * piece], 1, 1)
         back_pre = (gate * back * slope).astype(bf16)
         back_s[t] = back_pre
         gate_row = row_sums(act * back)
@@ -792,10 +806,10 @@
             jax.ShapeDtypeStruct((PIECES, piece, units), bf16),
             jax.ShapeDtypeStruct((units, width), bf16),
             jax.ShapeDtypeStruct((1, HALF), f32),
-            jax.ShapeDtypeStruct((8, FULL), i32),
+            jax.ShapeDtypeStruct((1,), i32),
         ),
         in_specs=[hbm, hbm, hbm, hbm, vmem, vmem, smem],
-        out_specs=(hbm, hbm, hbm, vmem, vmem),
+        out_specs=(hbm, hbm, hbm, vmem, smem),
         scratch_shapes=scratch,
         compiler_params=pltpu.CompilerParams(
             collective_id=0, has_side_effects=True, vmem_limit_bytes=60 * 2**20
@@ -807,7 +821,7 @@
 def local(*args):
     results = fast(*args)
     return lax.cond(
-        results[4][0, 0] <= 0, lambda found, args: found, lambda found, args: general(*args), results[:4], args
+        results[4][0] <= 0, lambda found, args: found, lambda found, args: general(*args), results[:4], args
     )
 
 

time: 209 us -> 197 us (0.943)
  Pallas kernels: 186 us -> 175 us
    pallas_call x1, Pallas kernels: 186 us -> 175 us  [fast(): pl.pallas_call(functools.partial(kernel, planes, experts), out_shape=(jax...]
where the time goes in v3:
time: 197 us
  Pallas kernels  175 us (89%)
  between operations  14.7 us (7%)
  local copies, waits for them, and re-layouts  6.93 us (4%)
    pallas_call x1, Pallas kernels, fast(): pl.pallas_call(functools.partial(kernel, planes, experts), out_shape=(jax...  175 us
    unnamed x16, local copies, waits for them, and re-layouts  6.93 us

profile of v3, /device:TPU:4, one launch (start us, length us, event | category | flops | bytes accessed | tf_op | source)
XLA Modules:
  0.0 197.3 jit_solution(9906608152959038767)
XLA Ops:
  7.2 0.0 copy-start
  7.2 0.0 copy-start.1
  7.2 0.0 copy-start.5
  7.2 0.0 copy-start.6
  7.2 0.0 copy-start.7
  7.2 175.4 %shard_map.110 = (bf16[128,2048]{1,0:T(8,128)(2,1)}, bf16[4,1024,256]{2,1,0:T(8,128)(2,1)}, bf16[256,4096]{1,0:T(8,128)(2,1)}, f32[1,64]{1,0:T(1,128)S(1)}, s32[1]{0:T(128)}) custom-call(bf16[128,4096]{1,0:T(8,128)(2,1)} %tokens.1, bf16[128,4096]{1,0:T(8,128)(2,1)} %cotangent.1, bf16[4,1024,256]{2,1,0:T(8,128)(2,1)} %bitcast.85, bf16[256,4096]{1,0:T(8,128)(2,1)} %bitcast.87, ...), custom_call_target="tpu_custom_call" | custom-call | tf_op jit(solution)/shard_map/pallas_call | solution.py:802
  183.3 0.0 copy-done
  183.3 0.0 copy-done.1
  183.3 0.0 copy-done.5
  183.3 0.0 copy-done.6
  183.3 0.0 copy-done.7
  183.3 0.2 conditional.1
  183.5 1.9 copy.35
  185.4 0.0 copy-start.4
  185.4 3.2 %copy.36 = bf16[1,4096,256]{2,1,0:T(8,128)(2,1)} copy(bf16[1,4096,256]{2,1,0:T(8,128)(2,1)} %get-tuple-element.88) | data formatting | bytes 4194304
  188.6 0.0 copy-done.4
  188.6 1.3 copy.37
  189.9 0.5 copy.38
Async XLA Ops:
  7.2 176.1 %copy-start = (bf16[128,4096]{1,0:T(8,128)(2,1)S(1)}, bf16[128,4096]{1,0:T(8,128)(2,1)}, u32[]{:S(2)}) copy-start(bf16[128,4096]{1,0:T(8,128)(2,1)} %tokens.1) | copy-start | bytes 3145732
  7.2 176.1 %copy-start.1 = (bf16[128,4096]{1,0:T(8,128)(2,1)S(1)}, bf16[128,4096]{1,0:T(8,128)(2,1)}, u32[]{:S(2)}) copy-start(bf16[128,4096]{1,0:T(8,128)(2,1)} %cotangent.1) | copy-start | bytes 3145732
  7.2 176.1 %copy-start.5 = (s32[16,1024]{1,0:T(8,128)S(1)}, s32[16,1024]{1,0:T(8,128)}, u32[]{:S(2)}) copy-start(s32[16,1024]{1,0:T(8,128)} %picks.1) | copy-start | bytes 196612
  7.2 176.1 %copy-start.6 = (f32[1,1024]{1,0:T(1,128)S(1)}, f32[1,1024]{1,0:T(1,128)}, u32[]{:S(2)}) copy-start(f32[1,1024]{1,0:T(1,128)} %gates.1) | copy-start | bytes 12292
  7.2 176.1 %copy-start.7 = (s32[16]{0:T(128)S(1)}, s32[16]{0:T(128)}, u32[]{:S(2)}) copy-start(s32[16]{0:T(128)} %counts.1) | copy-start | bytes 196
  185.4 3.2 %copy-start.4 = (bf16[1,256,4096]{2,1,0:T(8,128)(2,1)S(1)}, bf16[1,256,4096]{2,1,0:T(8,128)(2,1)}, u32[]{:S(2)}) copy-start(bf16[1,256,4096]{2,1,0:T(8,128)(2,1)} %get-tuple-element.89) | copy-start | bytes 6291460

commit v4 on v3

--- a/solution.py
+++ b/solution.py
@@ -17,133 +17,15 @@
     return (pre * normal_cdf, normal_cdf + pre * density)
 
 
-def general(tokens, cotangent, w_in, w_out, gates, picks, counts):
-    tok_dev, width = tokens.shape
-    patch_count = lax.axis_size("patch")
-    expert_count = lax.axis_size("expert")
-    hidden_parts = lax.axis_size("hidden")
-    capacity = picks.shape[1]
-    slots = capacity // patch_count
-    sources = patch_count * expert_count
-    bound = 2 * max(1, slots // sources)
-    limit = sources * bound
-    patch_here = lax.axis_index("patch")
-    expert_here = lax.axis_index("expert")
-    source_here = patch_here * expert_count + expert_here
-    slot_ids = jnp.arange(capacity, dtype=jnp.int32)
-    live = slot_ids[None, :] < counts[:, None]
-    holder = picks // tok_dev
-    local_row = picks % tok_dev
-    mine = (
-        ((holder == source_here) & live).reshape(expert_count, patch_count, slots).astype(jnp.int32)
-    )
-    order_mine = jnp.cumsum(mine, axis=2) - 1
-    expert_ids = jnp.arange(expert_count, dtype=jnp.int32)[:, None, None]
-    patch_ids = jnp.arange(patch_count, dtype=jnp.int32)[None, :, None]
-    position = (patch_ids * expert_count + expert_ids) * bound + order_mine
-    position = jnp.where(mine == 1, position, limit)
-    send_table = (
-        jnp.full((limit,), tok_dev, jnp.int32)
-        .at[position.reshape(-1)]
-        .set(local_row.reshape(-1), mode="drop")
-    )
-    send_rows = jnp.take(tokens, send_table, axis=0, mode="fill", fill_value=0).reshape(
-        sources, bound, width
-    )
-    send_grads = jnp.take(cotangent, send_table, axis=0, mode="fill", fill_value=0).reshape(
-        sources, bound, width
-    )
-    came_rows, came_grads = (
-        lax.all_to_all(send_rows, ("patch", "expert"), split_axis=0, concat_axis=0, tiled=True),
-        lax.all_to_all(send_grads, ("patch", "expert"), split_axis=0, concat_axis=0, tiled=True),
-    )
-    my_picks = lax.dynamic_slice_in_dim(picks, expert_here, 1, 0)[0]
-    block_picks = lax.dynamic_slice_in_dim(my_picks, patch_here * slots, slots, 0)
-    count_here = lax.dynamic_slice_in_dim(counts, expert_here, 1, 0)[0]
-    within = jnp.arange(slots, dtype=jnp.int32)
-    block_live = patch_here * slots + within < count_here
-    block_holder = block_picks // tok_dev
-    earlier_same = (
-        (block_holder[:, None] == block_holder[None, :])
-        & block_live[None, :]
-        & (within[None, :] < within[:, None])
-    )
-    block_order = jnp.sum(earlier_same.astype(jnp.int32), axis=1)
-    came_index = jnp.where(block_live, block_holder * bound + block_order, limit)
-    block_rows = jnp.take(
-        came_rows.reshape(limit, width), came_index, axis=0, mode="fill", fill_value=0
-    )
-    block_grads = jnp.take(
-        came_grads.reshape(limit, width), came_index, axis=0, mode="fill", fill_value=0
-    )
-    slot_rows, grad_rows = (
-        lax.all_gather(block_rows, "patch", axis=0, tiled=True),
-        lax.all_gather(block_grads, "patch", axis=0, tiled=True),
-    )
-    gate_col = gates[0][:, None]
-    weight_in = w_in[0]
-    weight_out = w_out[0]
-    unit_count = weight_in.shape[1]
-    pre = jnp.dot(slot_rows, weight_in, preferred_element_type=jnp.float32)
-    act, slope = gelu_parts(pre)
-    act_b = act.astype(jnp.bfloat16)
-    back_act = lax.dot_general(
-        grad_rows, weight_out, (((1,), (1,)), ((), ())), preferred_element_type=jnp.float32
-    )
-    gate_grad = jnp.sum(act * back_act, axis=1)
-    back_pre = (gate_col * back_act * slope).astype(jnp.bfloat16)
-    gated_rows = (gate_col * grad_rows.astype(jnp.float32)).astype(jnp.bfloat16)
-    grad_in = lax.dot_general(
-        slot_rows, back_pre, (((0,), (0,)), ((), ())), preferred_element_type=jnp.float32
-    )
-    grad_out = lax.dot_general(
-        act_b, gated_rows, (((0,), (0,)), ((), ())), preferred_element_type=jnp.float32
-    )
-    gate_terms = gate_grad.reshape(patch_count * hidden_parts, slots // hidden_parts)
-    d_gates = lax.psum_scatter(gate_terms, ("patch", "hidden"), scatter_dimension=0, tiled=True)
-    selector = (jnp.arange(tok_dev, dtype=jnp.int32)[:, None] == send_table[None, :]).astype(
-        jnp.bfloat16
-    )
-    back_blocks = back_pre.reshape(patch_count, slots, unit_count)
-    weight_halves = weight_in.reshape(hidden_parts, width // hidden_parts, unit_count)
-    slot_terms = jnp.einsum(
-        "psf,hdf->phsd", back_blocks, weight_halves, preferred_element_type=jnp.float32
-    ).astype(jnp.bfloat16)
-    slot_terms = slot_terms.reshape(patch_count * hidden_parts, slots, width // hidden_parts)
-    slot_sum = lax.psum_scatter(
-        slot_terms, ("patch", "hidden"), scatter_dimension=0, tiled=True
-    ).astype(jnp.float32)[0]
-    slot_grad = slot_sum.astype(jnp.bfloat16)
-    going_back = (
-        jnp.zeros((limit, width // hidden_parts), jnp.bfloat16)
-        .at[came_index]
-        .set(slot_grad, mode="drop")
-    )
-    send_width = width // hidden_parts
-    returned = lax.all_to_all(
-        going_back.reshape(sources, bound, send_width),
-        ("patch", "expert"),
-        split_axis=0,
-        concat_axis=0,
-        tiled=True,
-    )
-    returned = returned.reshape(limit, send_width)
-    token_grad = jnp.dot(selector, returned, preferred_element_type=jnp.float32)
-    d_tokens = token_grad.astype(jnp.bfloat16)
-    return (
-        d_tokens,
-        grad_in.astype(jnp.bfloat16)[None],
-        grad_out.astype(jnp.bfloat16)[None],
-        d_gates,
-    )
-
-
 MESH = pl.DeviceIdType.MESH
 f32 = jnp.float32
 bf16 = jnp.bfloat16
 i32 = jnp.int32
 PAIR = 16
 PIECES = 4
+OWN = PIECES // 2
+STRIDE = max(1, PIECES // 4)
+SUMS = 2
 CAP = 128
 HALF = CAP // 2
 SPILL = 32
@@ -192,6 +74,7 @@
     gates,
     picks,
     counts,
+    window,
     d_tok_hbm,
     d_in_hbm,
     d_out_hbm,
@@ -271,15 +154,15 @@
 
     loads = []
     for a, ref in enumerate((tokens, cotangent)):
-        for j in range(2):
-            col = pl.multiple_of((2 * c + j) * piece, piece)
+        for j in range(OWN):
+            col = pl.multiple_of((OWN * c + j) * piece, piece)
             cp = pltpu.make_async_copy(
-                ref.at[:, pl.ds(col, piece)], held.at[a, j], load_sem.at[2 * a + j]
+                ref.at[:, pl.ds(col, piece)], held.at[a, j], load_sem.at[OWN * a + j]
             )
             cp.start()
             loads.append(cp)
-    load_in = pltpu.make_async_copy(w_in_hbm, win, load_sem.at[4])
-    load_out = pltpu.make_async_copy(w_out_hbm, wout, load_sem.at[5])
+    load_in = pltpu.make_async_copy(w_in_hbm, win, load_sem.at[PIECES])
+    load_out = pltpu.make_async_copy(w_out_hbm, wout, load_sem.at[PIECES + 1])
     load_in.start()
     load_out.start()
 
@@ -298,7 +181,7 @@
         taken[pl.ds(i, 1), :] = contract(jnp.ones((8, FULL), bf16), folded.astype(bf16), 1, 1)[0:1]
         return carry
 
-    lax.fori_loop(0, experts, find, 0)
+    lax.fori_loop(0, experts, find, 0, unroll=4)
     present = taken[...]
     order = contract(present.astype(bf16), before, 1, 0)
     order = jnp.where(present > 0.5, order, -1.0).astype(i32)
@@ -369,7 +252,7 @@
         )
 
     def ring_up(a, j, t):
-        q = 2 * c + j
+        q = OWN * c + j
         return remote(
             allrows.at[a, q, t, pl.ds(0, HALF)],
             allrows.at[a, q, t + 1, pl.ds(0, HALF)],
@@ -379,7 +262,7 @@
         )
 
     def ring_down(a, j, t):
-        q = 2 * c + j
+        q = OWN * c + j
         return remote(
             allrows.at[a, q, t, pl.ds(HALF, HALF)],
             allrows.at[a, q, t + 1, pl.ds(HALF, HALF)],
@@ -389,7 +272,7 @@
         )
 
     def twin_copy(a, j, t):
-        q = 2 * c + j
+        q = OWN * c + j
         return remote(
             allrows.at[a, q, t],
             allrows.at[a, q, t],
@@ -423,15 +306,15 @@
         )
 
     for a in range(2):
-        for j in range(2):
-            loads[2 * a + j].wait()
+        for j in range(OWN):
+            loads[OWN * a + j].wait()
             going[a, j] = contract(pick_sel[...], held[a, j], 1, 0).astype(bf16)
             came[a, j, own_rows, :] = going[a, j, own_rows, :]
             for k in range(1, experts):
                 go_copy(a, j, k).start()
 
     def forward(p, t):
-        a, j = p // 2, p % 2
+        a, j = p // OWN, p % OWN
 
         @pl.when(t < planes)
         def _():
@@ -470,11 +353,14 @@
     live = so_far[planes - 1 : planes, :]
     excess = so_far - ((live * (group_row + 1)) >> 3)
     middle = (jnp.max(excess, axis=0, keepdims=True) + jnp.min(excess, axis=0, keepdims=True)) >> 1
-    flow = excess - middle
+    balanced = window[0] == 0
+    begin = jnp.maximum(window[0] - 1, 0) * CAP
+    flow = jnp.where(balanced, excess - middle, 0)
     rising = jnp.maximum(flow, 0)
     sinking = jnp.maximum(-flow, 0)
     risen = previous(rising)
     keep = amount - rising - previous(sinking)
+    keep = jnp.where(balanced, keep, jnp.clip(amount - begin, 0, CAP))
     up_at = following(keep)
     down_at = previous(keep + risen)
     for i, table in enumerate((keep, rising, risen, sinking)):
@@ -484,12 +370,15 @@
         return contract(grouped, x.astype(bf16), 0, 0)
 
     keep_s, rising_s = spread(keep), spread(rising)
-    dest = offsets + ranks - keep_s
+    dest = offsets + ranks - begin.astype(f32)
+    held_here = balanced | ((dest >= 0) & (dest < keep_s))
+    dest -= keep_s
     goes_up = (dest >= 0) & (dest < rising_s)
     goes_down = dest >= rising_s
     spot = jnp.where(
         dest < 0, dest + keep_s, jnp.where(goes_up, spread(up_at) + dest, spread(down_at) + dest - rising_s)
     )
+    spot = jnp.where(held_here, spot, -1.0)
     goes_down = (dest >= 0) & goes_down
     shift = jnp.where(goes_up, 1.0, jnp.where(goes_down, -1.0, 0.0))
 
@@ -501,16 +390,17 @@
     slot = per_slot(spot)
     block = ((mine >> 11) + per_slot(shift)) & (planes - 1)
     when = jnp.where(slot < HALF, z - block, block - z) & (planes - 1)
-    meta[0:1, :] = jnp.where(mine < 0, -1, when * CAP + slot)
+    unused = (mine < 0) | (slot < 0)
+    meta[0:1, :] = jnp.where(unused, -1, when * CAP + slot)
     meta[1:2, :] = block
-    meta[2:3, :] = jnp.where(mine < 0, -1, slot)
+    meta[2:3, :] = jnp.where(unused, -1, slot)
 
     own_group = pl.ds(pl.multiple_of(z * PAIR, PAIR), PAIR)
     widen = marks(iota((PAIR, pairs), 1) // PAIR == iota((PAIR, pairs), 0))
     start = contract(offs[own_group, :].astype(bf16), widen, 0, 0).astype(i32)
     size = contract(lens[own_group, :].astype(bf16), widen, 0, 0).astype(i32)
     index = iota((CAP, pairs), 1) & (PAIR - 1)
-    spot_here = jnp.where(index < size, start + index, -1)
+    spot_here = jnp.where(index < size, jnp.maximum(start + index - begin, -1), -1)
 
     def own(i):
         return tables[i, pl.ds(z, 1), :][:, 0:1]
@@ -550,33 +440,34 @@
     misfit[0] = jnp.max(bad)
 
     for a in range(2):
-        for j in range(2):
+        for j in range(OWN):
             came[a, j, pairs + 2 * SPILL :, :] = jnp.zeros((FULL - 2 * SPILL, piece), bf16)
     for a in range(2):
-        for j in range(2):
+        for j in range(OWN):
             for k in range(1, experts):
                 go_copy(a, j, k).wait()
             spilled[a, j] = contract(spill_sel[...], came[a, j, 0:pairs, :], 1, 0).astype(bf16)
             spill_up(a, j).start()
             spill_down(a, j).start()
-            for p in range(2 * a + j):
-                forward(p, 2 * a + j - p)
+            for p in range((OWN * a + j) % STRIDE, OWN * a + j, STRIDE):
+                forward(p, (OWN * a + j - p) // STRIDE)
             spill_up(a, j).wait()
             spill_down(a, j).wait()
-            allrows[a, 2 * c + j, 0] = contract(pack_sel[...], came[a, j], 1, 0).astype(bf16)
+            allrows[a, OWN * c + j, 0] = contract(pack_sel[...], came[a, j], 1, 0).astype(bf16)
             ring_up(a, j, 0).start()
             ring_down(a, j, 0).start()
             twin_copy(a, j, 0).start()
     load_in.wait()
     load_out.wait()
 
+    narrow = home.shape[2]
+
+    def weights(core, j):
+        begin = j * narrow
+        return win[OWN * core + begin // piece, begin % piece : begin % piece + narrow]
+
     def step(t, carry):
-        @pl.when(t > 0)
-        def _():
-            for p in range(3):
-                forward(p, t + 3 - p)
-
-        for j in range(2):
+        for j in range(OWN):
             twin_copy(0, j, t).wait_recv()
         pre = contract(allrows[0, 0, t], win[0], 1, 0)
         for q in range(1, PIECES):
@@ -591,9 +482,10 @@
 
         @pl.when(t > 0)
         def _():
-            forward(3, t)
-
-        for j in range(2):
+            for p in range(PIECES - STRIDE, PIECES):
+                forward(p, t)
+
+        for j in range(OWN):
             twin_copy(1, j, t).wait_recv()
         back = contract(allrows[1, 0, t], wout[:, 0:piece], 1, 1)
         for q in range(1, PIECES):
@@ -604,16 +496,18 @@
         gate_lo[pl.ds(lax.rem(z + planes - t, planes), 1), :] = gate_row
         gate_hi[pl.ds(lax.rem(z + t, planes), 1), :] = gate_row
 
-        for j in range(2):
+        for j in range(SUMS):
 
             @pl.when(t > 1)
             def _():
                 part_copy(j, t - 2).wait_send()
 
-            part_out[lax.rem(t, 2), j] = contract(back_pre, win[2 * other + j], 1, 1).astype(bf16)
+            part_out[lax.rem(t, 2), j] = contract(back_pre, weights(other, j), 1, 1).astype(bf16)
             part_copy(j, t).start()
-        for j in range(2):
-            own_part = contract(back_pre, win[2 * c + j], 1, 1)
+        for p in range(PIECES - STRIDE):
+            forward(p, t + 1 + (PIECES - 1 - p) // STRIDE)
+        for j in range(SUMS):
+            own_part = contract(back_pre, weights(c, j), 1, 1)
             part_copy(j, t).wait_recv()
             own_part += part_in[t, j].astype(f32)
 
@@ -661,7 +555,7 @@
         d_out[q] = contract(act_all, allrows[1, q].reshape(rows, piece), 0, 0).astype(bf16)
 
     last = planes - 1
-    for j in range(2):
+    for j in range(SUMS):
         sum_up(j, last).wait_recv()
         sum_down(j, last).wait_recv()
         slot_grad = (home[j] + sum_in[last, j].astype(f32)).astype(bf16)
@@ -707,24 +601,24 @@
     )
     d_gates[...] = jnp.where(c == 0, values[:, 0:HALF], values[:, HALF:])
 
-    for j in range(2):
+    for j in range(SUMS):
         for k in range(1, experts):
             grad_copy(j, k).wait()
         d_tok[j] = contract(pick_sel[...], grad_came[j], 0, 0).astype(bf16)
         cp = pltpu.make_async_copy(
-            d_tok.at[j], d_tok_hbm.at[:, pl.ds(j * piece, piece)], store_sem.at[2 * PIECES + j]
+            d_tok.at[j], d_tok_hbm.at[:, pl.ds(j * narrow, narrow)], store_sem.at[2 * PIECES + j]
         )
         cp.start()
         stores.append(cp)
 
     for a in range(2):
-        for j in range(2):
+        for j in range(OWN):
             for t in range(planes):
                 twin_copy(a, j, t).wait_send()
                 if t < planes - 1:
                     ring_up(a, j, t).wait_send()
                     ring_down(a, j, t).wait_send()
-    for j in range(2):
+    for j in range(SUMS):
         for t in (planes - 2, planes - 1):
             part_copy(j, t).wait_send()
             sum_up(j, t).wait_send()
@@ -733,13 +627,14 @@
         cp.wait()
 
 
-def fast(tokens, cotangent, w_in, w_out, gates, picks, counts):
+def layer(window, tokens, cotangent, w_in, w_out, gates, picks, counts):
     planes = lax.axis_size("patch")
     experts = lax.axis_size("expert")
     tok_dev, width = tokens.shape
     units = w_in.shape[2]
     capacity = picks.shape[1]
     piece = width // PIECES
+    narrow = width // 2 // SUMS
     pairs = experts * PAIR
     vmem = pl.BlockSpec(memory_space=pltpu.VMEM)
     smem = pl.BlockSpec(memory_space=pltpu.SMEM)
@@ -755,49 +650,49 @@
         pltpu.VMEM((pairs, tok_dev), bf16),
         pltpu.VMEM((CAP, pairs + FULL), bf16),
         pltpu.VMEM((2 * SPILL, pairs), bf16),
-        pltpu.VMEM((2, 2, tok_dev, piece), bf16),
-        pltpu.VMEM((2, 2, pairs, piece), bf16),
-        pltpu.VMEM((2, 2, pairs + FULL, piece), bf16),
-        pltpu.VMEM((2, 2, 2 * SPILL, piece), bf16),
+        pltpu.VMEM((2, OWN, tok_dev, piece), bf16),
+        pltpu.VMEM((2, OWN, pairs, piece), bf16),
+        pltpu.VMEM((2, OWN, pairs + FULL, piece), bf16),
+        pltpu.VMEM((2, OWN, 2 * SPILL, piece), bf16),
         pltpu.VMEM((2, PIECES, planes, CAP, piece), bf16),
         pltpu.VMEM((PIECES, piece, units), bf16),
         pltpu.VMEM((units, width), bf16),
         pltpu.VMEM((planes, CAP, units), bf16),
         pltpu.VMEM((planes, CAP, units), bf16),
-        pltpu.VMEM((2, CAP, piece), f32),
-        pltpu.VMEM((2, 2, CAP, piece), bf16),
-        pltpu.VMEM((planes, 2, CAP, piece), bf16),
-        pltpu.VMEM((2, 2, CAP, piece), bf16),
-        pltpu.VMEM((planes, 2, CAP, piece), bf16),
-        pltpu.VMEM((2, pairs + FULL, piece), bf16),
-        pltpu.VMEM((2, pairs, piece), bf16),
-        pltpu.VMEM((2, 2 * SPILL, piece), bf16),
-        pltpu.VMEM((2, tok_dev, piece), bf16),
+        pltpu.VMEM((SUMS, CAP, narrow), f32),
+        pltpu.VMEM((2, SUMS, CAP, narrow), bf16),
+        pltpu.VMEM((planes, SUMS, CAP, narrow), bf16),
+        pltpu.VMEM((2, SUMS, CAP, narrow), bf16),
+        pltpu.VMEM((planes, SUMS, CAP, narrow), bf16),
+        pltpu.VMEM((SUMS, pairs + FULL, narrow), bf16),
+        pltpu.VMEM((SUMS, pairs, narrow), bf16),
+        pltpu.VMEM((SUMS, 2 * SPILL, narrow), bf16),
+        pltpu.VMEM((SUMS, tok_dev, narrow), bf16),
         pltpu.VMEM((PIECES, piece, units), bf16),
         pltpu.VMEM((PIECES, units, piece), bf16),
         pltpu.VMEM((planes, CAP), f32),
         pltpu.VMEM((planes, CAP), f32),
         pltpu.VMEM((2 * planes, planes, CAP), f32),
-        dma((6,)),
-        dma((2, 2, experts)),
-        dma((2, 2, experts)),
-        dma((2, 2, 2)),
-        dma((2, 2, 2)),
-        dma((2, 2, 2, planes)),
-        dma((2, 2, 2, planes)),
-        dma((2, 2, planes)),
-        dma((2, 2, planes)),
-        dma((planes, 2)),
-        dma((planes, 2)),
-        dma((2, 2, planes)),
-        dma((2, 2, planes)),
-        dma((2, 2)),
-        dma((2, 2)),
-        dma((2, experts)),
-        dma((2, experts)),
+        dma((PIECES + 2,)),
+        dma((2, OWN, experts)),
+        dma((2, OWN, experts)),
+        dma((2, 2, OWN)),
+        dma((2, 2, OWN)),
+        dma((2, 2, OWN, planes)),
+        dma((2, 2, OWN, planes)),
+        dma((2, OWN, planes)),
+        dma((2, OWN, planes)),
+        dma((planes, SUMS)),
+        dma((planes, SUMS)),
+        dma((2, SUMS, planes)),
+        dma((2, SUMS, planes)),
+        dma((2, SUMS)),
+        dma((2, SUMS)),
+        dma((SUMS, experts)),
+        dma((SUMS, experts)),
         dma((2 * planes,)),
         dma((2 * planes,)),
-        dma((2 * PIECES + 2,)),
+        dma((2 * PIECES + SUMS,)),
     ]
     d_tokens, d_in, d_out, d_gates, misfit = pl.pallas_call(
         functools.partial(kernel, planes, experts),
@@ -808,21 +703,67 @@
             jax.ShapeDtypeStruct((1, HALF), f32),
             jax.ShapeDtypeStruct((1,), i32),
         ),
-        in_specs=[hbm, hbm, hbm, hbm, vmem, vmem, smem],
+        in_specs=[hbm, hbm, hbm, hbm, vmem, vmem, smem, smem],
         out_specs=(hbm, hbm, hbm, vmem, smem),
         scratch_shapes=scratch,
         compiler_params=pltpu.CompilerParams(
             collective_id=0, has_side_effects=True, vmem_limit_bytes=60 * 2**20
         ),
-    )(tokens, cotangent, w_in.reshape(PIECES, piece, units), w_out[0], gates, picks, counts)
+    )(
+        tokens,
+        cotangent,
+        w_in.reshape(PIECES, piece, units),
+        w_out[0],
+        gates,
+        picks,
+        counts,
+        jnp.reshape(window, (1,)).astype(i32),
+    )
     return (d_tokens, d_in.reshape(w_in.shape), d_out[None], d_gates, misfit)
 
 
+def store(*refs):
+    count = (len(refs) - 2) // 3
+    came_sem, went_sem = refs[-2:]
+    arriving, leaving = [], []
+    for src, dst, mid in zip(refs[:count], refs[count : 2 * count], refs[2 * count :]):
+        parts = 4 if src.shape[-2] > FULL else 1
+        rows = src.shape[-2] // parts
+        for i in range(parts):
+            at = pl.ds(i * rows, rows)
+            cut = (slice(None), at) if len(src.shape) > 2 else (at,)
+            n = len(arriving)
+            arriving.append(pltpu.make_async_copy(src.at[cut], mid.at[cut], came_sem.at[n]))
+            leaving.append(pltpu.make_async_copy(mid.at[cut], dst.at[cut], went_sem.at[n]))
+    for cp in arriving:
+        cp.start()
+    for first, second in zip(arriving, leaving):
+        first.wait()
+        second.start()
+    for cp in leaving:
+        cp.wait()
+
+
 def local(*args):
-    results = fast(*args)
-    return lax.cond(
-        results[4][0] <= 0, lambda found, args: found, lambda found, args: general(*args), results[:4], args
-    )
+    results = layer(0, *args)
+
+    def windows(found, args):
+        def add(i, total):
+            part = layer(i + 1, *args)[:4]
+            return tuple((x.astype(f32) + y.astype(f32)).astype(x.dtype) for x, y in zip(total, part))
+
+        return lax.fori_loop(0, 2, add, tuple(jnp.zeros_like(x) for x in found))
+
+    results = lax.cond(results[4][0] <= 0, lambda found, args: found, windows, results[:4], args)
+    hbm = pl.BlockSpec(memory_space=pl.ANY)
+    return pl.pallas_call(
+        store,
+        out_shape=tuple(jax.ShapeDtypeStruct(x.shape, x.dtype) for x in results),
+        in_specs=[hbm] * 4,
+        out_specs=(hbm,) * 4,
+        scratch_shapes=[pltpu.VMEM(x.shape, x.dtype) for x in results]
+        + [pltpu.SemaphoreType.DMA((12,))] * 2,
+    )(*results)
 
 
 def solution(mesh):

time: 197 us -> 181 us (0.919)
  between operations: 14.7 us -> 1.52 us
  local copies, waits for them, and re-layouts: 6.93 us -> 0.02 us
  Pallas kernels: 175 us -> 179 us
    unnamed x16 -> x10, local copies, waits for them, and re-layouts: 6.93 us -> 0.02 us
    pallas_call x1 -> x2, Pallas kernels: 175 us -> 179 us  [the longest x1 174 us: layer(): pl.pallas_call(functools.partial(kernel, planes, experts), out_shape=(jax...]
where the time goes in v4:
time: 181 us; the launch traced here: 180 us
  Pallas kernels  179 us (99%)
    pallas_call x1, Pallas kernels, layer(): pl.pallas_call(functools.partial(kernel, planes, experts), out_shape=(jax...  174 us
    pallas_call x1, Pallas kernels, local(): pl.pallas_call(store, out_shape=tuple((jax.ShapeDtypeStruct(x.shape, x.dt...  4.21 us

profile of v4, /device:TPU:4, one launch (start us, length us, event | category | flops | bytes accessed | tf_op | source)
XLA Modules:
  0.0 180.4 jit_solution(6881125106252050659)
XLA Ops:
  0.6 0.0 copy-start
  0.6 0.0 copy-start.4
  0.7 0.0 copy-start.7
  0.7 0.0 copy-start.8
  0.7 0.0 copy-start.9
  0.7 174.4 %shard_map.102 = (bf16[128,2048]{1,0:T(8,128)(2,1)}, bf16[4,1024,256]{2,1,0:T(8,128)(2,1)}, bf16[256,4096]{1,0:T(8,128)(2,1)}, f32[1,64]{1,0:T(1,128)}, s32[1]{0:T(128)}) custom-call(bf16[128,4096]{1,0:T(8,128)(2,1)} %tokens.1, bf16[128,4096]{1,0:T(8,128)(2,1)} %cotangent.1, bf16[4,1024,256]{2,1,0:T(8,128)(2,1)} %bitcast.25, bf16[256,4096]{1,0:T(8,128)(2,1)} %bitcast.27, ...), custom_call_target="tpu_custom_call" | custom-call | tf_op jit(solution)/shard_map/pallas_call | solution.py:697
  175.7 0.0 copy-done
  175.8 0.0 copy-done.4
  175.8 0.0 copy-done.7
  175.8 0.0 copy-done.8
  175.8 0.0 copy-done.9
  175.8 0.2 conditional.1
  176.0 4.2 %shard_map.103 = (bf16[128,2048]{1,0:T(8,128)(2,1)}, bf16[1,4096,256]{2,1,0:T(8,128)(2,1)}, bf16[1,256,4096]{2,1,0:T(8,128)(2,1)}, f32[1,64]{1,0:T(1,128)}) custom-call(bf16[128,2048]{1,0:T(8,128)(2,1)} %get-tuple-element.253.refs_0_, bf16[1,4096,256]{2,1,0:T(8,128)(2,1)} %get-tuple-element.254.refs_1_, bf16[1,256,4096]{2,1,0:T(8,128)(2,1)} %get-tuple-element.255.refs_2_, ...), custom_call_target="tpu_custom_call" | custom-call | tf_op jit(solution)/shard_map/pallas_call | solution.py:759
Async XLA Ops:
  0.6 175.1 %copy-start = (bf16[1,4096,256]{2,1,0:T(8,128)(2,1)S(1)}, bf16[1,4096,256]{2,1,0:T(8,128)(2,1)}, u32[]{:S(2)}) copy-start(bf16[1,4096,256]{2,1,0:T(8,128)(2,1)} %param.13) | copy-start | bytes 6291460
  0.6 175.1 %copy-start.4 = (bf16[128,4096]{1,0:T(8,128)(2,1)S(1)}, bf16[128,4096]{1,0:T(8,128)(2,1)}, u32[]{:S(2)}) copy-start(bf16[128,4096]{1,0:T(8,128)(2,1)} %tokens.1) | copy-start | bytes 3145732
  0.7 175.1 %copy-start.7 = (s32[16,1024]{1,0:T(8,128)S(1)}, s32[16,1024]{1,0:T(8,128)}, u32[]{:S(2)}) copy-start(s32[16,1024]{1,0:T(8,128)} %picks.1) | copy-start | bytes 196612
  0.7 175.1 %copy-start.8 = (f32[1,1024]{1,0:T(1,128)S(1)}, f32[1,1024]{1,0:T(1,128)}, u32[]{:S(2)}) copy-start(f32[1,1024]{1,0:T(1,128)} %gates.1) | copy-start | bytes 12292
  0.7 175.1 %copy-start.9 = (s32[16]{0:T(128)S(1)}, s32[16]{0:T(128)}, u32[]{:S(2)}) copy-start(s32[16]{0:T(128)} %counts.1) | copy-start | bytes 196

commit v5 on v4

--- a/solution.py
+++ b/solution.py
@@ -551,8 +551,12 @@
 
     rows = planes * CAP
     act_all = act_s[...].reshape(rows, act_s.shape[2])
-    for q in range(PIECES):
+
+    def out_piece(q, carry):
         d_out[q] = contract(act_all, allrows[1, q].reshape(rows, piece), 0, 0).astype(bf16)
+        return carry
+
+    lax.fori_loop(0, PIECES, out_piece, 0)
 
     last = planes - 1
     for j in range(SUMS):
@@ -579,9 +583,14 @@
         cp.start()
         stores.append(cp)
     back_all = back_s[...].reshape(rows, back_s.shape[2])
-    for q in range(PIECES):
+
+    def in_piece(q, carry):
         turned = contract(back_all, allrows[0, q].reshape(rows, piece), 0, 0)
         d_in[q] = turned.T.astype(bf16)
+        return carry
+
+    lax.fori_loop(0, PIECES, in_piece, 0)
+    for q in range(PIECES):
         cp = pltpu.make_async_copy(d_in.at[q], d_in_hbm.at[q], store_sem.at[PIECES + q])
         cp.start()
         stores.append(cp)

time: 181 us -> 181 us (level)
  no operation moved by 1% of the time
where the time goes in v5:
time: 181 us; the launch traced here: 180 us
  Pallas kernels  179 us (99%)
    pallas_call x1, Pallas kernels, layer(): pl.pallas_call(functools.partial(kernel, planes, experts), out_shape=(jax...  174 us
    pallas_call x1, Pallas kernels, local(): pl.pallas_call(store, out_shape=tuple((jax.ShapeDtypeStruct(x.shape, x.dt...  4.21 us

profile of v5, /device:TPU:4, one launch (start us, length us, event | category | flops | bytes accessed | tf_op | source)
XLA Modules:
  0.0 180.4 jit_solution(6213313315477591171)
XLA Ops:
  0.6 0.0 copy-start
  0.6 0.0 copy-start.4
  0.7 0.0 copy-start.7
  0.7 0.0 copy-start.8
  0.7 0.0 copy-start.9
  0.7 174.5 %shard_map.102 = (bf16[128,2048]{1,0:T(8,128)(2,1)}, bf16[4,1024,256]{2,1,0:T(8,128)(2,1)}, bf16[256,4096]{1,0:T(8,128)(2,1)}, f32[1,64]{1,0:T(1,128)}, s32[1]{0:T(128)}) custom-call(bf16[128,4096]{1,0:T(8,128)(2,1)} %tokens.1, bf16[128,4096]{1,0:T(8,128)(2,1)} %cotangent.1, bf16[4,1024,256]{2,1,0:T(8,128)(2,1)} %bitcast.25, bf16[256,4096]{1,0:T(8,128)(2,1)} %bitcast.27, ...), custom_call_target="tpu_custom_call" | custom-call | tf_op jit(solution)/shard_map/pallas_call | solution.py:706
  175.8 0.0 copy-done
  175.8 0.0 copy-done.4
  175.8 0.0 copy-done.7
  175.8 0.0 copy-done.8
  175.8 0.0 copy-done.9
  175.8 0.2 conditional.1
  176.0 4.2 %shard_map.103 = (bf16[128,2048]{1,0:T(8,128)(2,1)}, bf16[1,4096,256]{2,1,0:T(8,128)(2,1)}, bf16[1,256,4096]{2,1,0:T(8,128)(2,1)}, f32[1,64]{1,0:T(1,128)}) custom-call(bf16[128,2048]{1,0:T(8,128)(2,1)} %get-tuple-element.253.refs_0_, bf16[1,4096,256]{2,1,0:T(8,128)(2,1)} %get-tuple-element.254.refs_1_, bf16[1,256,4096]{2,1,0:T(8,128)(2,1)} %get-tuple-element.255.refs_2_, ...), custom_call_target="tpu_custom_call" | custom-call | tf_op jit(solution)/shard_map/pallas_call | solution.py:768
Async XLA Ops:
  0.6 175.1 %copy-start = (bf16[1,4096,256]{2,1,0:T(8,128)(2,1)S(1)}, bf16[1,4096,256]{2,1,0:T(8,128)(2,1)}, u32[]{:S(2)}) copy-start(bf16[1,4096,256]{2,1,0:T(8,128)(2,1)} %param.13) | copy-start | bytes 6291460
  0.6 175.1 %copy-start.4 = (bf16[128,4096]{1,0:T(8,128)(2,1)S(1)}, bf16[128,4096]{1,0:T(8,128)(2,1)}, u32[]{:S(2)}) copy-start(bf16[128,4096]{1,0:T(8,128)(2,1)} %tokens.1) | copy-start | bytes 3145732
  0.7 175.1 %copy-start.7 = (s32[16,1024]{1,0:T(8,128)S(1)}, s32[16,1024]{1,0:T(8,128)}, u32[]{:S(2)}) copy-start(s32[16,1024]{1,0:T(8,128)} %picks.1) | copy-start | bytes 196612
  0.7 175.1 %copy-start.8 = (f32[1,1024]{1,0:T(1,128)S(1)}, f32[1,1024]{1,0:T(1,128)}, u32[]{:S(2)}) copy-start(f32[1,1024]{1,0:T(1,128)} %gates.1) | copy-start | bytes 12292
  0.7 175.1 %copy-start.9 = (s32[16]{0:T(128)S(1)}, s32[16]{0:T(128)}, u32[]{:S(2)}) copy-start(s32[16]{0:T(128)} %counts.1) | copy-start | bytes 196
